TPU v7x, 32 devices: a whole 2x2x4 slice. The times are simulated.
32 devices in a mesh: ctx: 4 (over y, core), exp: 8 (over z, x).
Axes of the slice: x: 2, y: 2, z: 4, core: 2. Of those that a mesh axis runs over, the one named last changes fastest.
Arguments:
- residual: bfloat16 [8, 512, 7168], P('exp', 'ctx'), may hold values from -6 to 6
- queries: bfloat16 [8, 512, 1024], P('exp', 'ctx'), may hold values from -64 to 64
- latent: bfloat16 [8, 512, 512], P('exp', 'ctx'), may hold values from -6 to 6
- out_proj: bfloat16 [1024, 7168], P('ctx'), may hold values from -0.5 to 0.5
- up_weight: bfloat16 [8, 7168, 1024], P('exp', 'ctx'), may hold values from -0.0625 to 0.0625
- down_weight: bfloat16 [8, 1024, 7168], P('exp', None, 'ctx'), may hold values from -0.1875 to 0.1875
- cotangent: bfloat16 [8, 512, 7168], P('exp', 'ctx'), may hold values from -6 to 6
- routes: int32 [8, 512, 8], P('exp', 'ctx'), may hold values from 0 to 255, as said below
- gate_values: float32 [8, 512, 8], P('exp', 'ctx'), may hold values from 0.2 to 1
- documents: int32 [8, 4], P('exp'), may hold values from 0 to 2, never falling along the last dimension, each value on 1 to 2 neighbouring positions
Outputs:
- layer_out: bfloat16 [8, 512, 7168], P('exp', 'ctx')
- input_grad: bfloat16 [8, 512, 7168], P('exp', 'ctx')
- up_grad: bfloat16 [8, 7168, 1024], P('exp', 'ctx')
- down_grad: bfloat16 [8, 1024, 7168], P('exp', None, 'ctx')
Inputs may be any that keep to these rules, and one draw needn't show every extreme that they name: Each token's 8 experts differ. Within one block of 128 consecutive tokens of a sequence at most 4 routes name one expert below 8, and in every draw some expert below 8 is named by exactly 4 routes of every such block. `documents`: document numbers never fall along a sequence; a document covers 1 to 2 consecutive blocks, and one covers exactly 2.
All inputs are finite; a program needn't handle non-finite values.
Results may differ from a plain program's by a relative error of at most 0.025.
Values may be sent and summed in bfloat16 or wider, within the bound.
A program may use at most 128 MiB of HBM per device.

v0:
```python
import math

import jax
import jax.numpy as jnp
from jax import lax
from jax.sharding import PartitionSpec as P

LAT = 512
HEADS = 2
CAP = 4
BLOCK = 128


def shifted(shard, axis, by):
    peers = lax.axis_size(axis)
    pairs = [(i, i + by) for i in range(peers) if 0 <= i + by < peers]
    return lax.ppermute(shard, axis, pairs)


def silu_grad(values_in):
    sigmoid_of = jax.nn.sigmoid(values_in)
    return sigmoid_of * (1.0 + values_in * (1.0 - sigmoid_of))


def slot_tables(route_rows, gate_rows, expert_total, capacity):
    experts = jnp.arange(expert_total, dtype=jnp.int32)
    onehot = (route_rows[:, :, None] == experts[None, None, :]).astype(jnp.int32)
    flat_hits = onehot.reshape(-1, expert_total)
    before = jnp.cumsum(flat_hits, axis=0) - flat_hits
    rank_in = jnp.sum(before * flat_hits, axis=1).reshape(route_rows.shape)
    valid = route_rows < expert_total
    slot_index = jnp.where(valid, route_rows * capacity + rank_in, -1)
    slots_all = jnp.arange(expert_total * capacity, dtype=jnp.int32)
    slot_hits = slot_index[None, :, :] == slots_all[:, None, None]
    picker = jnp.sum(slot_hits.astype(jnp.float32), axis=2)
    weigher = jnp.sum(jnp.where(slot_hits, gate_rows[None, :, :], 0.0), axis=2)
    return (picker, weigher)


def shards(
    residual,
    queries,
    latent,
    out_proj,
    up_weight,
    down_weight,
    cotangent,
    routes,
    gate_values,
    documents,
):
    ctx_count = lax.axis_size("ctx")
    exp_count = lax.axis_size("exp")
    my_index = lax.axis_index("ctx")
    tokens = residual.shape[1]
    model_width = residual.shape[2]
    doc_row = documents[0]
    block_total = doc_row.shape[0]
    inv_root = 1.0 / math.sqrt(LAT)
    query_rows = queries[0].reshape(tokens, HEADS, LAT)
    token_iota = jnp.arange(tokens, dtype=jnp.int32)
    block_iota = jnp.arange(block_total, dtype=jnp.int32)

    def doc_of(positions):
        matches = (positions // BLOCK)[:, None] == block_iota[None, :]
        return jnp.sum(jnp.where(matches, doc_row[None, :], 0), axis=1)

    query_pos = my_index * tokens + token_iota
    query_doc = doc_of(query_pos)

    def fold_keys(running_max, running_sum, weighted, key_block, source):
        key_pos = source * tokens + token_iota
        allowed = (
            (query_doc[:, None] == doc_of(key_pos)[None, :])
            & (key_pos[None, :] <= query_pos[:, None])
            & (source >= 0)
        )
        scores = (
            jnp.einsum("thk,jk->thj", query_rows, key_block, preferred_element_type=jnp.float32)
            * inv_root
        )
        scores = jnp.where(allowed[:, None, :], scores, -1e30)
        new_max = jnp.maximum(running_max, jnp.max(scores, axis=2))
        exponent = jnp.where(allowed[:, None, :], jnp.exp(scores - new_max[:, :, None]), 0.0)
        rescale = jnp.exp(running_max - new_max)
        running_sum = running_sum * rescale + jnp.sum(exponent, axis=2)
        weighted = weighted * rescale[:, :, None] + jnp.einsum(
            "thj,jk->thk",
            exponent.astype(jnp.bfloat16),
            key_block,
            preferred_element_type=jnp.float32,
        )
        return (new_max, running_sum, weighted)

    start_max = jnp.full((tokens, HEADS), -1e30, jnp.float32)
    start_sum = jnp.zeros((tokens, HEADS), jnp.float32)
    start_acc = jnp.zeros((tokens, HEADS, LAT), jnp.float32)
    first_max, first_sum, first_acc = fold_keys(
        start_max, start_sum, start_acc, latent[0], my_index
    )
    cycle_turns = ctx_count - 1

    def cycle_turn(cycle_step, loop_carry):
        key_block, running_max, running_sum, weighted = loop_carry
        key_block = shifted(key_block, "ctx", 1)
        running_max, running_sum, weighted = fold_keys(
            running_max, running_sum, weighted, key_block, my_index - cycle_step
        )
        return (key_block, running_max, running_sum, weighted)

    loop_carry = lax.fori_loop(
        1, cycle_turns + 1, cycle_turn, (latent[0], first_max, first_sum, first_acc)
    )
    heads_out = (
        (loop_carry[3] / loop_carry[2][:, :, None])
        .astype(jnp.bfloat16)
        .reshape(tokens, HEADS * LAT)
    )
    projected = jnp.dot(
        heads_out,
        lax.all_gather(out_proj, "ctx", axis=0, tiled=True),
        preferred_element_type=jnp.float32,
    )
    hidden_in = (residual[0].astype(jnp.float32) + projected).astype(jnp.bfloat16)
    picker, weigher = slot_tables(routes[0], gate_values[0], exp_count, CAP)
    picker_half = picker.astype(jnp.bfloat16)
    slot_gate = jnp.sum(weigher, axis=1)
    slot_in = jnp.dot(picker_half, hidden_in, preferred_element_type=jnp.float32).astype(
        jnp.bfloat16
    )
    slot_cot = (
        jnp.dot(picker_half, cotangent[0], preferred_element_type=jnp.float32) * slot_gate[:, None]
    ).astype(jnp.bfloat16)
    slot_in = slot_in.reshape(1, exp_count, CAP, model_width)
    slot_cot = slot_cot.reshape(1, exp_count, CAP, model_width)
    arrived_in, arrived_cot = (
        lax.all_to_all(
            lax.all_to_all(slot_in, "ctx", split_axis=3, concat_axis=0, tiled=True),
            "exp",
            split_axis=1,
            concat_axis=1,
            tiled=True,
        ),
        lax.all_to_all(
            lax.all_to_all(slot_cot, "ctx", split_axis=3, concat_axis=0, tiled=True),
            "exp",
            split_axis=1,
            concat_axis=1,
            tiled=True,
        ),
    )
    part_width = model_width // ctx_count
    row_total = ctx_count * exp_count * CAP
    in_rows = arrived_in.reshape(row_total, part_width)
    cot_rows = arrived_cot.reshape(row_total, part_width)
    up_part = up_weight[0]
    down_part = down_weight[0]
    contract_rows = (((0,), (0,)), ((), ()))
    contract_cols = (((1,), (1,)), ((), ()))

    def sum_all(term_rows):
        return lax.psum(term_rows.astype(jnp.bfloat16), "ctx").astype(jnp.float32)

    pre_full = sum_all(jnp.dot(in_rows, up_part, preferred_element_type=jnp.float32))
    activated = jax.nn.silu(pre_full).astype(jnp.bfloat16)
    grad_full = sum_all(
        lax.dot_general(cot_rows, down_part, contract_cols, preferred_element_type=jnp.float32)
    )
    pre_grad = (grad_full * silu_grad(pre_full)).astype(jnp.bfloat16)
    slot_out = jnp.dot(activated, down_part, preferred_element_type=jnp.float32).astype(
        jnp.bfloat16
    )
    down_grad = lax.dot_general(
        activated, cot_rows, contract_rows, preferred_element_type=jnp.float32
    ).astype(jnp.bfloat16)
    up_grad = lax.dot_general(
        in_rows, pre_grad, contract_rows, preferred_element_type=jnp.float32
    ).astype(jnp.bfloat16)
    slot_in_grad = lax.dot_general(
        pre_grad, up_part, contract_cols, preferred_element_type=jnp.float32
    ).astype(jnp.bfloat16)
    returned_out, returned_grad = (
        lax.all_to_all(
            lax.all_to_all(
                slot_out.reshape(ctx_count, exp_count, CAP, part_width),
                "ctx",
                split_axis=0,
                concat_axis=3,
                tiled=True,
            ),
            "exp",
            split_axis=1,
            concat_axis=1,
            tiled=True,
        ),
        lax.all_to_all(
            lax.all_to_all(
                slot_in_grad.reshape(ctx_count, exp_count, CAP, part_width),
                "ctx",
                split_axis=0,
                concat_axis=3,
                tiled=True,
            ),
            "exp",
            split_axis=1,
            concat_axis=1,
            tiled=True,
        ),
    )
    flat_out = returned_out.reshape(exp_count * CAP, model_width).astype(jnp.float32)
    flat_grad = returned_grad.reshape(exp_count * CAP, model_width).astype(jnp.float32)
    gathered_out = lax.dot_general(
        weigher,
        flat_out,
        contract_rows,
        precision=lax.Precision.HIGHEST,
        preferred_element_type=jnp.float32,
    )
    gathered_grad = lax.dot_general(
        picker,
        flat_grad,
        contract_rows,
        precision=lax.Precision.HIGHEST,
        preferred_element_type=jnp.float32,
    )
    layer_out = (hidden_in.astype(jnp.float32) + gathered_out).astype(jnp.bfloat16)
    input_grad = (cotangent[0].astype(jnp.float32) + gathered_grad).astype(jnp.bfloat16)
    return (layer_out[None], input_grad[None], up_grad[None], down_grad[None])


def solution(mesh):
    placed = (
        P("exp", "ctx", None),
        P("exp", "ctx", None),
        P("exp", "ctx", None),
        P("ctx", None),
        P("exp", "ctx", None),
        P("exp", None, "ctx"),
        P("exp", "ctx", None),
        P("exp", "ctx", None),
        P("exp", "ctx", None),
        P("exp", None),
    )
    return jax.shard_map(
        shards,
        mesh=mesh,
        in_specs=placed,
        out_specs=(
            P("exp", "ctx", None),
            P("exp", "ctx", None),
            P("exp", "ctx", None),
            P("exp", None, "ctx"),
        ),
        check_vma=False,
    )
```

profile of v0, /device:TPU:0, one launch (start us, length us, event | category | flops | bytes accessed | tf_op | source)
XLA Modules:
  0.0 325.2 jit_solution(8045653405223786688)
XLA Ops:
  7.2 1.0 copy.162
  8.6 2.3 reduce-window.6
  10.9 0.3 slice_reduce_fusion
  11.6 0.3 select_reduce_fusion.1
  11.9 0.4 fusion.21
  12.5 7.3 %copy.124 = bf16[1,8,4,7168]{1,2,0,3:T(4,128)(2,1)} copy(bf16[1,8,4,7168]{3,2,1,0:T(4,128)(2,1)S(1)} %reshape.229) | data formatting | bytes 917504 | tf_op jit(solution)/shard_map/reshape | solution.py:135
  19.8 10.5 %reshape.241 = bf16[4,2,28672]{2,1,0:T(2,128)(2,1)} reshape(bf16[7168,1,4,8]{3,2,1,0:T(4,128)(2,1)} %bitcast.119) | data formatting | bytes 917504
  30.3 4.2 %all-to-all-start.4 = ((bf16[4,2,28672]{2,1,0:T(2,128)(2,1)}), bf16[4,2,28672]{2,1,0:T(2,128)(2,1)S(1)}, u32[]{:S(2)}, u32[]{:S(2)}) async-start(bf16[4,2,28672]{2,1,0:T(2,128)(2,1)} %reshape.241), calls=%async_computation.4 | async-start | bytes 917504 | tf_op jit(solution)/shard_map/all_to_all | solution.py:145
  35.3 0.3 convolution_add_fusion.4
  35.6 28.1 %while.22 = (s32[]{:T(128)}, bf16[128,512]{1,0:T(8,128)(2,1)S(1)}, f32[128,2]{0,1:T(2,128)S(1)}, f32[128,2]{0,1:T(2,128)S(1)}, f32[128,2,512]{2,0,1:T(8,128)S(1)...) while((s32[]{:T(128)}, bf16[128,512]{1,0:T(8,128)(2,1)S(1)}, ...), condition=%wide.region_7.8_spmd.clone, body=%wide.region_3.7_spmd.clone.sunk | while | flops 67735680 | bytes 2839267 | solution.py:111
  35.6 2.4 collective-permute-start
  38.3 0.7 collective-permute-done
  39.0 0.2 fusion.97
  39.3 0.3 convolution_add_fusion.6
  39.7 12.6 %collective-permute-start = (bf16[128,512]{1,0:T(8,128)(2,1)S(1)}, bf16[128,512]{1,0:T(8,128)(2,1)S(1)}, u32[]{:S(2)}, u32[]{:S(2)}) collective-permute-start(bf16[128,512]{1,0:T(8,128)(2,1)S(1)} %get-tuple-element.493), channel_id=1, source_target_pairs={{0,8},{8,16},{16,24},{1,9},{9,17},{17,25},{2,10},{10,18},{18,26},{... | collective-permute-start | bytes 393224 | tf_op jit(solution)/shard_map/while/body/eval_jaxpr/ppermute | solution.py:17
  52.6 0.7 collective-permute-done
  53.3 0.2 fusion.97
  53.6 0.3 convolution_add_fusion.6
  54.0 8.1 %collective-permute-start = (bf16[128,512]{1,0:T(8,128)(2,1)S(1)}, bf16[128,512]{1,0:T(8,128)(2,1)S(1)}, u32[]{:S(2)}, u32[]{:S(2)}) collective-permute-start(bf16[128,512]{1,0:T(8,128)(2,1)S(1)} %get-tuple-element.493), channel_id=1, source_target_pairs={{0,8},{8,16},{16,24},{1,9},{9,17},{17,25},{2,10},{10,18},{18,26},{... | collective-permute-start | bytes 393224 | tf_op jit(solution)/shard_map/while/body/eval_jaxpr/ppermute | solution.py:17
  62.3 0.7 collective-permute-done
  63.4 0.3 convolution_add_fusion.6
  64.0 47.4 %all-gather.2.cloned.1.call-done = bf16[1024,7168]{1,0:T(8,128)(2,1)} async-done(((bf16[256,7168]{1,0:T(8,128)(2,1)}), bf16[1024,7168]{1,0:T(8,128)(2,1)}) %all-gather.2.cloned.1.call-update) | async-done | bytes 14680080 | tf_op jit(solution)/shard_map/all_gather | solution.py:121
  111.4 8.3 %fusion.16 = bf16[128,7168]{1,0:T(8,128)(2,1)S(1)} fusion(bf16[128,1024]{0,1:T(8,128)(2,1)S(1)} %bitcast.127, bf16[1024,7168]{1,0:T(8,128)(2,1)} %all-gather.2.cloned.1.call-done, bf16[1,128,7168]{2,1,0:T(8,128)(2,1)} %param.12), kind=kOutput, calls=%fused_computation.29 | convolution fusion | flops 1881800704 | bytes 18612224 | tf_op jit(solution)/shard_map/dot_general | solution.py:119
  119.6 0.4 convolution_convert_fusion
  120.2 7.3 %copy.117 = bf16[1,8,4,7168]{1,2,0,3:T(4,128)(2,1)} copy(bf16[1,8,4,7168]{3,2,1,0:T(4,128)(2,1)S(1)} %reshape.225) | data formatting | bytes 917504 | tf_op jit(solution)/shard_map/reshape | solution.py:134
  127.5 10.1 %reshape.239 = bf16[4,2,28672]{2,1,0:T(2,128)(2,1)} reshape(bf16[7168,1,4,8]{3,2,1,0:T(4,128)(2,1)} %bitcast.120) | data formatting | bytes 917504
  137.5 5.7 %all-to-all-start = ((bf16[4,2,28672]{2,1,0:T(2,128)(2,1)}), bf16[4,2,28672]{2,1,0:T(2,128)(2,1)S(1)}, u32[]{:S(2)}, u32[]{:S(2)}) async-start(bf16[4,2,28672]{2,1,0:T(2,128)(2,1)} %reshape.239), calls=%async_computation | async-start | bytes 917504 | tf_op jit(solution)/shard_map/all_to_all | solution.py:138
  143.2 9.8 %reshape.242 = bf16[7168,1,4,8]{3,2,1,0:T(4,128)(2,1)} reshape(bf16[4,2,28672]{2,1,0:T(2,128)(2,1)S(1)} %all-to-all-done.4) | data formatting | bytes 917504
  153.0 11.3 %copy.126 = bf16[4,8,4,1792]{3,0,2,1:T(4,128)(2,1)} copy(bf16[4,8,4,1792]{1,2,3,0:T(4,128)(2,1)} %bitcast.121) | data formatting | bytes 917504 | tf_op jit(solution)/shard_map/all_to_all | solution.py:145
  164.3 5.8 %all-to-all-start.5 = ((bf16[4,8,4,1792]{3,0,2,1:T(4,128)(2,1)}), bf16[4,8,4,1792]{3,0,2,1:T(4,128)(2,1)S(1)}, u32[]{:S(2)}, u32[]{:S(2)}) async-start(bf16[4,8,4,1792]{3,0,2,1:T(4,128)(2,1)} %copy.126), calls=%async_computation.5 | async-start | bytes 917504 | tf_op jit(solution)/shard_map/all_to_all | solution.py:144
  170.1 9.8 %reshape.240 = bf16[7168,1,4,8]{3,2,1,0:T(4,128)(2,1)} reshape(bf16[4,2,28672]{2,1,0:T(2,128)(2,1)S(1)} %all-to-all-done) | data formatting | bytes 917504
  179.9 11.3 %copy.119 = bf16[4,8,4,1792]{3,0,2,1:T(4,128)(2,1)} copy(bf16[4,8,4,1792]{1,2,3,0:T(4,128)(2,1)} %bitcast.122) | data formatting | bytes 917504 | tf_op jit(solution)/shard_map/all_to_all | solution.py:138
  191.2 6.0 %all-to-all-start.1 = ((bf16[4,8,4,1792]{3,0,2,1:T(4,128)(2,1)}), bf16[4,8,4,1792]{3,0,2,1:T(4,128)(2,1)S(1)}, u32[]{:S(2)}, u32[]{:S(2)}) async-start(bf16[4,8,4,1792]{3,0,2,1:T(4,128)(2,1)} %copy.119), calls=%async_computation.1 | async-start | bytes 917504 | tf_op jit(solution)/shard_map/all_to_all | solution.py:137
  197.2 0.9 copy.127
  198.1 1.1 reshape.230
  199.3 4.0 %fusion.42 = bf16[128,1024]{1,0:T(8,128)(2,1)} fusion(bf16[128,1792]{1,0:T(8,128)(2,1)S(1)} %reshape.230, bf16[1,1024,1792]{2,1,0:T(8,128)(2,1)} %param.17), kind=kOutput, calls=%fused_computation.54 | convolution fusion | flops 469893120 | bytes 4390912 | tf_op jit(solution)/shard_map/dot_general | solution.py:167
  203.3 7.0 %all-to-all-done.1 = bf16[4,8,4,1792]{3,0,2,1:T(4,128)(2,1)S(1)} async-done(((bf16[4,8,4,1792]{3,0,2,1:T(4,128)(2,1)}), bf16[4,8,4,1792]{3,0,2,1:T(4,128)(2,1)S(1)}, u32[]{:S(2)}, u32[]{:S(2)}) %all-to-all-start.1) | async-done | bytes 458784 | tf_op jit(solution)/shard_map/all_to_all | solution.py:137
  210.3 0.9 copy.120
  211.3 1.1 reshape.226
  212.4 3.4 %fusion.39 = bf16[128,1024]{1,0:T(8,128)(2,1)} fusion(bf16[128,1792]{1,0:T(8,128)(2,1)S(1)} %reshape.226, bf16[1,1792,1024]{2,1,0:T(8,128)(2,1)} %param.16), kind=kOutput, calls=%fused_computation.53 | convolution fusion | flops 469893120 | bytes 4390912 | tf_op jit(solution)/shard_map/dot_general | solution.py:164
  215.8 33.1 %all-reduce.3.cloned.1.call-done = (bf16[128,1024]{1,0:T(8,128)(2,1)}, bf16[128,1024]{1,0:T(8,128)(2,1)}) async-done(((bf16[128,1024]{1,0:T(8,128)(2,1)}, bf16[128,1024]{1,0:T(8,128)(2,1)}), (bf16[128,1024]{1,0:T(8,128)(2,1)}, bf16[128,1024]{1,0:T(8,128)(2,1)})) %all-reduce.3.cloned.1.call-update) | async-done | bytes 524304 | tf_op jit(solution)/shard_map/psum | solution.py:162
  248.9 4.4 %fusion.32 = bf16[128,1792]{1,0:T(8,128)(2,1)} fusion(bf16[1,1792,1024]{2,1,0:T(8,128)(2,1)} %param.16, bf16[128,1024]{1,0:T(8,128)(2,1)} %get-tuple-element.392, bf16[128,1024]{1,0:T(8,128)(2,1)} %get-tuple-element.393), kind=kOutput, calls=%fused_computation.49 | convolution fusion | flops 471433216 | bytes 4653056 | tf_op jit(solution)/shard_map/dot_general | solution.py:179
  253.3 1.1 reshape.231
  254.4 0.8 copy.128
  255.2 3.5 %all-to-all-start.6 = ((bf16[4,8,4,1792]{3,1,2,0:T(8,128)(2,1)}), bf16[4,8,4,1792]{3,1,2,0:T(8,128)(2,1)S(1)}, u32[]{:S(2)}, u32[]{:S(2)}) async-start(bf16[4,8,4,1792]{3,1,2,0:T(8,128)(2,1)} %copy.128), calls=%async_computation.6 | async-start | bytes 917504 | tf_op jit(solution)/shard_map/all_to_all | solution.py:197
  258.7 3.5 %fusion.35 = bf16[128,1792]{1,0:T(8,128)(2,1)} fusion(bf16[1,1024,1792]{2,1,0:T(8,128)(2,1)} %param.17, bf16[128,1024]{1,0:T(8,128)(2,1)S(1)} %copy-done.1), kind=kOutput, calls=%fused_computation.50 | convolution fusion | flops 470777856 | bytes 4390912 | tf_op jit(solution)/shard_map/dot_general | solution.py:170
  262.2 1.9 reshape.227
  264.1 1.8 copy.121
  266.0 0.9 all-to-all-done.6
  266.8 4.1 %all-to-all-start.2 = ((bf16[4,8,4,1792]{3,1,2,0:T(8,128)(2,1)}), bf16[4,8,4,1792]{3,1,2,0:T(8,128)(2,1)}, u32[]{:S(2)}, u32[]{:S(2)}) async-start(bf16[4,8,4,1792]{3,1,2,0:T(8,128)(2,1)} %copy.121), calls=%async_computation.2 | async-start | bytes 917504 | tf_op jit(solution)/shard_map/all_to_all | solution.py:184
  271.0 1.1 copy.139
  272.1 2.0 reshape.237
  274.0 5.1 %all-to-all-done.2 = bf16[4,8,4,1792]{3,1,2,0:T(8,128)(2,1)} async-done(((bf16[4,8,4,1792]{3,1,2,0:T(8,128)(2,1)}), bf16[4,8,4,1792]{3,1,2,0:T(8,128)(2,1)}, u32[]{:S(2)}, u32[]{:S(2)}) %all-to-all-start.2) | async-done | bytes 458784 | tf_op jit(solution)/shard_map/all_to_all | solution.py:184
  279.2 5.5 %all-to-all-start.7 = ((bf16[1,8,4,7168]{3,2,0,1:T(4,128)(2,1)}), bf16[1,8,4,7168]{3,2,0,1:T(4,128)(2,1)S(1)}, u32[]{:S(2)}, u32[]{:S(2)}) async-start(bf16[1,8,4,7168]{3,2,0,1:T(4,128)(2,1)} %reshape.237), calls=%async_computation.7 | async-start | bytes 917504 | tf_op jit(solution)/shard_map/all_to_all | solution.py:196
  284.7 2.1 copy.136
  286.8 2.0 reshape.236
  288.8 8.8 %all-to-all-done.7 = bf16[1,8,4,7168]{3,2,0,1:T(4,128)(2,1)S(1)} async-done(((bf16[1,8,4,7168]{3,2,0,1:T(4,128)(2,1)}), bf16[1,8,4,7168]{3,2,0,1:T(4,128)(2,1)S(1)}, u32[]{:S(2)}, u32[]{:S(2)}) %all-to-all-start.7) | async-done | bytes 458784 | tf_op jit(solution)/shard_map/all_to_all | solution.py:196
  297.6 4.3 %all-to-all-start.3 = ((bf16[1,8,4,7168]{3,2,0,1:T(4,128)(2,1)}), bf16[1,8,4,7168]{3,2,0,1:T(4,128)(2,1)}, u32[]{:S(2)}, u32[]{:S(2)}) async-start(bf16[1,8,4,7168]{3,2,0,1:T(4,128)(2,1)} %reshape.236), calls=%async_computation.3 | async-start | bytes 917504 | tf_op jit(solution)/shard_map/all_to_all | solution.py:183
  302.0 3.0 fusion.31
  305.0 3.0 fusion.30
  308.1 4.4 %fusion.19 = bf16[1,128,7168]{2,1,0:T(8,128)(2,1)} fusion(f32[32,128]{1,0:T(8,128)S(1)} %get-tuple-element.371, bf16[32,7168]{1,0:T(8,128)(2,1)S(1)} %reshape.232, bf16[1,128,7168]{2,1,0:T(8,128)(2,1)} %param.18), kind=kOutput, calls=%fused_computation.32 | convolution fusion | flops 355074048 | bytes 4145152 | tf_op jit(solution)/shard_map/dot_general | solution.py:219
  312.6 1.7 all-to-all-done.3
  314.3 1.1 reshape.228
  315.4 2.9 fusion.20
  (73 shorter events, 3.4 us)
Async XLA Ops:
  7.2 4.8 %copy-start = (bf16[1,128,7168]{2,1,0:T(8,128)(2,1)S(1)}, bf16[1,128,7168]{2,1,0:T(8,128)(2,1)}, u32[]{:S(2)}) copy-start(bf16[1,128,7168]{2,1,0:T(8,128)(2,1)} %param.18) | copy-start | bytes 5505028
  7.2 1.1 copy-start.4
  7.2 4.4 %copy-start.5 = (f32[1,128,8]{1,2,0:T(8,128)S(1)}, f32[1,128,8]{1,2,0:T(8,128)}, u32[]{:S(2)}) copy-start(f32[1,128,8]{1,2,0:T(8,128)} %param.20) | copy-start | bytes 12292
  7.2 104.2 %all-gather.2.cloned.1.call-start = ((), (), s32[]{:S(2)}) async-start(), calls=%async_computation.8 | async-start | bytes 18350080 | tf_op jit(solution)/shard_map/all_gather | solution.py:121
  19.8 14.7 %copy-start.3 = (bf16[1,128,1024]{2,1,0:T(8,128)(2,1)S(1)}, bf16[1,128,1024]{2,1,0:T(8,128)(2,1)}, u32[]{:S(2)}) copy-start(bf16[1,128,1024]{2,1,0:T(8,128)(2,1)} %param.13) | copy-start | bytes 786436
  19.8 15.1 %copy-start.6 = (s32[1,4]{1,0:T(1,128)S(1)}, s32[1,4]{1,0:T(1,128)}, u32[]{:S(2)}) copy-start(s32[1,4]{1,0:T(1,128)} %param.21) | copy-start | bytes 52
  30.3 107.2 %all-to-all-start.4 = ((bf16[4,2,28672]{2,1,0:T(2,128)(2,1)}), bf16[4,2,28672]{2,1,0:T(2,128)(2,1)S(1)}, u32[]{:S(2)}, u32[]{:S(2)}) async-start(bf16[4,2,28672]{2,1,0:T(2,128)(2,1)} %reshape.241), calls=%async_computation.4 | async-start | bytes 917504 | tf_op jit(solution)/shard_map/all_to_all | solution.py:145
  35.6 3.4 %collective-permute-start = (bf16[128,512]{1,0:T(8,128)(2,1)S(1)}, bf16[128,512]{1,0:T(8,128)(2,1)S(1)}, u32[]{:S(2)}, u32[]{:S(2)}) collective-permute-start(bf16[128,512]{1,0:T(8,128)(2,1)S(1)} %get-tuple-element.493), channel_id=1, source_target_pairs={{0,8},{8,16},{16,24},{1,9},{9,17},{17,25},{2,10},{10,18},{18,26},{... | collective-permute-start | bytes 393224 | tf_op jit(solution)/shard_map/while/body/eval_jaxpr/ppermute | solution.py:17
  39.7 13.6 %collective-permute-start = (bf16[128,512]{1,0:T(8,128)(2,1)S(1)}, bf16[128,512]{1,0:T(8,128)(2,1)S(1)}, u32[]{:S(2)}, u32[]{:S(2)}) collective-permute-start(bf16[128,512]{1,0:T(8,128)(2,1)S(1)} %get-tuple-element.493), channel_id=1, source_target_pairs={{0,8},{8,16},{16,24},{1,9},{9,17},{17,25},{2,10},{10,18},{18,26},{... | collective-permute-start | bytes 393224 | tf_op jit(solution)/shard_map/while/body/eval_jaxpr/ppermute | solution.py:17
  54.0 9.1 %collective-permute-start = (bf16[128,512]{1,0:T(8,128)(2,1)S(1)}, bf16[128,512]{1,0:T(8,128)(2,1)S(1)}, u32[]{:S(2)}, u32[]{:S(2)}) collective-permute-start(bf16[128,512]{1,0:T(8,128)(2,1)S(1)} %get-tuple-element.493), channel_id=1, source_target_pairs={{0,8},{8,16},{16,24},{1,9},{9,17},{17,25},{2,10},{10,18},{18,26},{... | collective-permute-start | bytes 393224 | tf_op jit(solution)/shard_map/while/body/eval_jaxpr/ppermute | solution.py:17
  137.5 26.8 %all-to-all-start = ((bf16[4,2,28672]{2,1,0:T(2,128)(2,1)}), bf16[4,2,28672]{2,1,0:T(2,128)(2,1)S(1)}, u32[]{:S(2)}, u32[]{:S(2)}) async-start(bf16[4,2,28672]{2,1,0:T(2,128)(2,1)} %reshape.239), calls=%async_computation | async-start | bytes 917504 | tf_op jit(solution)/shard_map/all_to_all | solution.py:138
  164.3 26.9 %all-to-all-start.5 = ((bf16[4,8,4,1792]{3,0,2,1:T(4,128)(2,1)}), bf16[4,8,4,1792]{3,0,2,1:T(4,128)(2,1)S(1)}, u32[]{:S(2)}, u32[]{:S(2)}) async-start(bf16[4,8,4,1792]{3,0,2,1:T(4,128)(2,1)} %copy.126), calls=%async_computation.5 | async-start | bytes 917504 | tf_op jit(solution)/shard_map/all_to_all | solution.py:144
  191.2 19.2 %all-to-all-start.1 = ((bf16[4,8,4,1792]{3,0,2,1:T(4,128)(2,1)}), bf16[4,8,4,1792]{3,0,2,1:T(4,128)(2,1)S(1)}, u32[]{:S(2)}, u32[]{:S(2)}) async-start(bf16[4,8,4,1792]{3,0,2,1:T(4,128)(2,1)} %copy.119), calls=%async_computation.1 | async-start | bytes 917504 | tf_op jit(solution)/shard_map/all_to_all | solution.py:137
  197.1 51.7 %all-reduce.3.cloned.1.call-start = ((), (), s32[]{:S(2)}) async-start(), calls=%async_computation.9 | async-start | bytes 1048576 | tf_op jit(solution)/shard_map/psum | solution.py:162
  248.9 9.8 %copy-start.1 = (bf16[128,1024]{1,0:T(8,128)(2,1)S(1)}, bf16[128,1024]{1,0:T(8,128)(2,1)}, u32[]{:S(2)}) copy-start(bf16[128,1024]{1,0:T(8,128)(2,1)} %get-tuple-element.392) | copy-start | bytes 786436
  255.2 11.6 %all-to-all-start.6 = ((bf16[4,8,4,1792]{3,1,2,0:T(8,128)(2,1)}), bf16[4,8,4,1792]{3,1,2,0:T(8,128)(2,1)S(1)}, u32[]{:S(2)}, u32[]{:S(2)}) async-start(bf16[4,8,4,1792]{3,1,2,0:T(8,128)(2,1)} %copy.128), calls=%async_computation.6 | async-start | bytes 917504 | tf_op jit(solution)/shard_map/all_to_all | solution.py:197
  266.8 12.3 %all-to-all-start.2 = ((bf16[4,8,4,1792]{3,1,2,0:T(8,128)(2,1)}), bf16[4,8,4,1792]{3,1,2,0:T(8,128)(2,1)}, u32[]{:S(2)}, u32[]{:S(2)}) async-start(bf16[4,8,4,1792]{3,1,2,0:T(8,128)(2,1)} %copy.121), calls=%async_computation.2 | async-start | bytes 917504 | tf_op jit(solution)/shard_map/all_to_all | solution.py:184
  279.2 18.4 %all-to-all-start.7 = ((bf16[1,8,4,7168]{3,2,0,1:T(4,128)(2,1)}), bf16[1,8,4,7168]{3,2,0,1:T(4,128)(2,1)S(1)}, u32[]{:S(2)}, u32[]{:S(2)}) async-start(bf16[1,8,4,7168]{3,2,0,1:T(4,128)(2,1)} %reshape.237), calls=%async_computation.7 | async-start | bytes 917504 | tf_op jit(solution)/shard_map/all_to_all | solution.py:196
  297.6 16.7 %all-to-all-start.3 = ((bf16[1,8,4,7168]{3,2,0,1:T(4,128)(2,1)}), bf16[1,8,4,7168]{3,2,0,1:T(4,128)(2,1)}, u32[]{:S(2)}, u32[]{:S(2)}) async-start(bf16[1,8,4,7168]{3,2,0,1:T(4,128)(2,1)} %reshape.236), calls=%async_computation.3 | async-start | bytes 917504 | tf_op jit(solution)/shard_map/all_to_all | solution.py:183
  302.0 3.0 copy-start.2
Sparse Core Ops, SparseCore 0:
  9.6 101.7 all-gather.1
  215.9 32.8 all-reduce.2
where the time goes:
time: 327 us; the launch traced here: 325 us
  waiting for transfers between devices  106 us (32%)
  local copies, waits for them, and re-layouts  98.2 us (30%)
  starting transfers between devices  62.2 us (19%)
  matrix products  40 us (12%)
  between operations  14.3 us (4%)
  other arithmetic  4.02 us (1%)
    all_gather x1, waiting for transfers between devices, shards(): lax.all_gather(out_proj, 'ctx', axis=0, tiled=True)  47.4 us
    unnamed x22, local copies, waits for them, and re-layouts  41.8 us
    psum x1, waiting for transfers between devices, sum_all(): return lax.psum(term_rows.astype(jnp.bfloat16), 'ctx').astype(jnp.float32)  33.1 us
    ppermute x3, starting transfers between devices, shifted(): return lax.ppermute(shard, axis, pairs)  23.2 us
    all_to_all x1, local copies, waits for them, and re-layouts, shards(): lax.all_to_all(slot_cot, 'ctx', split_axis=3, concat_axis=0, tiled=True)  11.3 us
    all_to_all x1, local copies, waits for them, and re-layouts, shards(): lax.all_to_all(slot_in, 'ctx', split_axis=3, concat_axis=0, tiled=True)  11.3 us
    all_to_all x1, waiting for transfers between devices, shards(): lax.all_to_all(lax.all_to_all(slot_in_grad.reshape(ctx_count, exp_count,...  8.83 us
    dot_general x1, matrix products, shards(): jnp.dot(heads_out, lax.all_gather(out_proj, 'ctx', axis=0, tiled=True), p...  8.26 us
  transfers between devices with their start and end apart: 13, of which 10 were waited for; matrix products, arithmetic and copies ran while one was open for 39% of the time, Pallas kernels for 0%

commit v1 on v0

v1 whole, which is shorter than its diff:
```python
import functools
import math

import jax
import jax.numpy as jnp
from jax import lax
from jax.experimental import pallas as pl
from jax.experimental.pallas import tpu as pltpu
from jax.sharding import PartitionSpec as P

LAT = 512
HEADS = 2
CAP = 4
BLOCK = 128
MSG = 16
MESH = pl.DeviceIdType.MESH


def group_of(kind):
    ctx_count = lax.axis_size("ctx")
    exp_count = lax.axis_size("exp")
    c = lax.axis_index("ctx")
    e = lax.axis_index("exp")
    if kind == "all":
        return (
            ctx_count * exp_count,
            c * exp_count + e,
            lambda j: (j // exp_count, j % exp_count),
        )
    if kind == "ctx":
        return ctx_count, c, lambda j: (j, e)
    if kind == "core":
        return 2, c % 2, lambda j: ((c // 2) * 2 + j, e)
    return ctx_count // 2, c // 2, lambda j: (j * 2 + c % 2, e)


def exchange_kernel(kind, same, send_ref, out_ref, send_sem, recv_sem, own_sem):
    n, me, place = group_of(kind)
    barrier = pltpu.get_barrier_semaphore()

    def greet(k, carry):
        pl.semaphore_signal(
            barrier, inc=1, device_id=place((me + k) % n), device_id_type=MESH
        )
        return carry

    lax.fori_loop(1, n, greet, 0)
    pl.semaphore_wait(barrier, n - 1)

    def copy_to(k):
        peer = (me + k) % n
        return pltpu.make_async_remote_copy(
            src_ref=send_ref if same else send_ref.at[peer],
            dst_ref=out_ref.at[me],
            send_sem=send_sem.at[k],
            recv_sem=recv_sem.at[k],
            device_id=place(peer),
            device_id_type=MESH,
        )

    def start(k, carry):
        copy_to(k).start()
        return carry

    def finish(k, carry):
        copy_to(k).wait()
        return carry

    lax.fori_loop(1, n, start, 0)
    own = pltpu.make_async_copy(
        send_ref if same else send_ref.at[me], out_ref.at[me], own_sem
    )
    own.start()
    own.wait()
    lax.fori_loop(1, n, finish, 0)


def exchange(kind, send, same, collective_id):
    n = group_of(kind)[0]
    block = send.shape if same else send.shape[1:]
    return pl.pallas_call(
        functools.partial(exchange_kernel, kind, same),
        out_shape=jax.ShapeDtypeStruct((n,) + tuple(block), send.dtype),
        in_specs=[pl.BlockSpec(memory_space=pl.ANY)],
        out_specs=pl.BlockSpec(memory_space=pl.ANY),
        scratch_shapes=[
            pltpu.SemaphoreType.DMA((n,)),
            pltpu.SemaphoreType.DMA((n,)),
            pltpu.SemaphoreType.DMA,
        ],
        compiler_params=pltpu.CompilerParams(
            collective_id=collective_id, has_side_effects=True
        ),
    )(send)


def dot32(a, b):
    return jnp.dot(a, b, preferred_element_type=jnp.float32)


def dims(a, b, contract):
    return lax.dot_general(a, b, (contract, ((), ())), preferred_element_type=jnp.float32)


def head_slice(queries, latent, doc_row, width):
    ctx_count = lax.axis_size("ctx")
    tokens = latent.shape[0]
    length = ctx_count * tokens
    send = jnp.stack(
        [
            jnp.concatenate(
                [latent, queries[:, (j * width // LAT) * LAT : (j * width // LAT + 1) * LAT]]
            )
            for j in range(ctx_count)
        ]
    )
    got = exchange("ctx", send, False, 1)
    keys = got[:, :tokens].reshape(length, LAT)
    asks = got[:, tokens:].reshape(length, LAT)
    positions = jnp.arange(length, dtype=jnp.int32)
    owner = jnp.repeat(doc_row, BLOCK, total_repeat_length=length)
    allowed = (owner[:, None] == owner[None, :]) & (positions[None, :] <= positions[:, None])
    scores = dims(asks, keys, ((1,), (1,))) * (1.0 / math.sqrt(LAT))
    scores = jnp.where(allowed, scores, -1e30)
    largest = jnp.max(scores, axis=1, keepdims=True)
    expo = jnp.where(allowed, jnp.exp(scores - largest), 0.0)
    total = jnp.sum(expo, axis=1, keepdims=True)
    first = (lax.axis_index("ctx") * width) % LAT
    values = lax.dynamic_slice(keys, (0, first), (length, width))
    return (dot32(expo.astype(jnp.bfloat16), values) / total).astype(jnp.bfloat16)


def slot_tables(route_rows, gate_rows, experts):
    tokens = route_rows.shape[0]
    named = route_rows[None, :, :] == jnp.arange(experts, dtype=jnp.int32)[:, None, None]
    hit = jnp.sum(named.astype(jnp.float32), axis=2)
    gate = jnp.sum(jnp.where(named, gate_rows[None, :, :], 0.0), axis=2)
    at = jnp.arange(tokens, dtype=jnp.int32)
    earlier = (at[:, None] < at[None, :]).astype(jnp.bfloat16)
    before = dot32(hit.astype(jnp.bfloat16), earlier)
    slots = jnp.arange(CAP, dtype=jnp.float32)
    picked = (hit[:, None, :] > 0.5) & (before[:, None, :] == slots[None, :, None])
    picker = picked.astype(jnp.float32).reshape(experts * CAP, tokens)
    weigher = jnp.where(picked, gate[:, None, :], 0.0).reshape(experts * CAP, tokens)
    return picker, weigher


def shards(
    residual,
    queries,
    latent,
    out_proj,
    up_weight,
    down_weight,
    cotangent,
    routes,
    gate_values,
    documents,
):
    ctx_count = lax.axis_size("ctx")
    experts = lax.axis_size("exp")
    tokens = residual.shape[1]
    model = residual.shape[2]
    chips = ctx_count // 2
    part = model // ctx_count
    half = part // 2
    rows = experts * CAP
    bf16 = jnp.bfloat16

    width = out_proj.shape[0]
    heads = head_slice(queries[0], latent[0], documents[0], width)
    heads = heads.reshape(chips, 2, tokens, width).swapaxes(0, 1)
    partial_sums = dot32(heads.reshape(-1, width), out_proj).astype(bf16)
    paired = exchange("core", partial_sums.reshape(2, chips * tokens, model), False, 2)
    paired = (paired[0].astype(jnp.float32) + paired[1].astype(jnp.float32)).astype(bf16)
    landed = exchange("chip", paired.reshape(chips, tokens, model), False, 3)
    projected = jnp.sum(landed.astype(jnp.float32), axis=0)
    hidden_in = (residual[0].astype(jnp.float32) + projected).astype(bf16)

    picker, weigher = slot_tables(routes[0], gate_values[0], experts)
    picker_half = picker.astype(bf16)
    slot_gate = jnp.sum(weigher, axis=1)
    slot_in = dot32(picker_half, hidden_in).astype(bf16)
    slot_cot = (dot32(picker_half, cotangent[0]) * slot_gate[:, None]).astype(bf16)

    to_row = jnp.arange(experts * MSG, dtype=jnp.int32)
    from_row = ((to_row % MSG) // CAP) * rows + (to_row // MSG) * CAP + to_row % CAP
    order = (from_row[:, None] == to_row[None, :]).astype(bf16)

    def pack(first, second):
        return jnp.einsum(
            "pq,gqw->gpw", order, jnp.concatenate([first[0], first[1], second[0], second[1]], axis=1),
            preferred_element_type=jnp.float32,
        ).astype(bf16).reshape(ctx_count * experts, MSG, half)

    def unpack(messages):
        return jnp.einsum(
            "qp,gqw->gpw", order, messages.reshape(ctx_count, experts * MSG, half),
            preferred_element_type=jnp.float32,
        ).astype(bf16)

    def by_part(values):
        return [
            jnp.stack(
                [values[:, j * part + h * half : j * part + (h + 1) * half] for j in range(ctx_count)]
            )
            for h in range(2)
        ]

    arrived = unpack(exchange("all", pack(by_part(slot_in), by_part(slot_cot)), False, 4))

    def joined(values, first):
        pieces = [
            values[:, (first + h) * rows : (first + h + 1) * rows].reshape(ctx_count * rows, half)
            for h in range(2)
        ]
        return jnp.concatenate(pieces, axis=1)

    in_rows = joined(arrived, 0)
    cot_rows = joined(arrived, 2)
    up_part = up_weight[0]
    down_part = down_weight[0]
    hidden = up_part.shape[1]

    pre_part = dot32(in_rows, up_part).astype(bf16).reshape(ctx_count, rows, hidden)
    act_part = dims(cot_rows, down_part, ((1,), (1,))).astype(bf16)
    act_part = act_part.reshape(ctx_count, rows, hidden)
    terms = exchange("ctx", jnp.concatenate([pre_part, act_part], axis=1), False, 5)
    sums = jnp.sum(terms.astype(jnp.float32), axis=0)
    pre = sums[:rows]
    act_grad = sums[rows:]
    sig = jax.nn.sigmoid(pre)
    own_act = jax.nn.silu(pre).astype(bf16)
    own_grad = (act_grad * (sig * (1.0 + pre * (1.0 - sig)))).astype(bf16)
    units = exchange("ctx", jnp.concatenate([own_act, own_grad]), True, 6)
    activated = units[:, :rows].reshape(ctx_count * rows, hidden)
    pre_grad = units[:, rows:].reshape(ctx_count * rows, hidden)

    slot_out = dot32(activated, down_part).astype(bf16)
    slot_in_grad = dims(pre_grad, up_part, ((1,), (1,))).astype(bf16)
    down_grad = dims(activated, cot_rows, ((0,), (0,))).astype(bf16)
    up_grad = dims(in_rows, pre_grad, ((0,), (0,))).astype(bf16)

    def halves(values):
        grouped = values.reshape(ctx_count, rows, part)
        return [grouped[:, :, :half], grouped[:, :, half:]]

    back = unpack(exchange("all", pack(halves(slot_out), halves(slot_in_grad)), False, 7))

    def widened(first):
        return jnp.concatenate(
            [
                back[j, (first + h) * rows : (first + h + 1) * rows]
                for j in range(ctx_count)
                for h in range(2)
            ],
            axis=1,
        )

    flat_out = widened(0)
    flat_grad = widened(2)
    high = weigher.astype(bf16)
    low = (weigher - high.astype(jnp.float32)).astype(bf16)
    gathered_out = dims(
        jnp.concatenate([high, low]), jnp.concatenate([flat_out, flat_out]), ((0,), (0,))
    )
    gathered_grad = dims(picker_half, flat_grad, ((0,), (0,)))
    layer_out = (hidden_in.astype(jnp.float32) + gathered_out).astype(bf16)
    input_grad = (cotangent[0].astype(jnp.float32) + gathered_grad).astype(bf16)
    return (layer_out[None], input_grad[None], up_grad[None], down_grad[None])


def solution(mesh):
    placed = (
        P("exp", "ctx", None),
        P("exp", "ctx", None),
        P("exp", "ctx", None),
        P("ctx", None),
        P("exp", "ctx", None),
        P("exp", None, "ctx"),
        P("exp", "ctx", None),
        P("exp", "ctx", None),
        P("exp", "ctx", None),
        P("exp", None),
    )
    return jax.shard_map(
        shards,
        mesh=mesh,
        in_specs=placed,
        out_specs=(
            P("exp", "ctx", None),
            P("exp", "ctx", None),
            P("exp", "ctx", None),
            P("exp", None, "ctx"),
        ),
        check_vma=False,
    )
```

time: 327 us -> 322 us (0.985)
  Pallas kernels: 0 us -> 255 us
  waiting for transfers between devices: 106 us -> 0 us
  local copies, waits for them, and re-layouts: 98.2 us -> 9.98 us
  starting transfers between devices: 62.2 us -> 0 us
  other arithmetic: 4.02 us -> 19.3 us
  between operations: 14.3 us -> 1.03 us
  matrix products: 40 us -> 36.1 us
    pallas_call x0 -> x7, Pallas kernels: none -> 255 us  [exchange(): pl.pallas_call(functools.partial(exchange_kernel, kind, same), out_shape=...]
    all_gather x1 -> x0, waiting for transfers between devices: 47.4 us -> none  [shards(): lax.all_gather(out_proj, 'ctx', axis=0, tiled=True)]
    all_to_all x8 -> x0, starting transfers between devices: 39 us -> none  [the longest x1 5.98 us: shards(): lax.all_to_all(lax.all_to_all(slot_in, 'ctx', split_axis=3, concat_axis=0...]
    unnamed x22 -> x31, local copies, waits for them, and re-layouts: 41.8 us -> 5.54 us
    psum x1 -> x0, waiting for transfers between devices: 33.1 us -> none  [sum_all(): return lax.psum(term_rows.astype(jnp.bfloat16), 'ctx').astype(jnp.float32)]
    all_to_all x8 -> x0, local copies, waits for them, and re-layouts: 31.6 us -> none  [the longest x1 11.3 us: shards(): lax.all_to_all(slot_cot, 'ctx', split_axis=3, concat_axis=0, tiled=True)]
    reshape x14 -> x1, local copies, waits for them, and re-layouts: 24.2 us -> 0.02 us  [shards(): heads = heads.reshape(chips, 2, tokens, width).swapaxes(0, 1)]
    all_to_all x8 -> x0, waiting for transfers between devices: 23.6 us -> none  [the longest x1 8.83 us: shards(): lax.all_to_all(lax.all_to_all(slot_in_grad.reshape(ctx_count, exp_count,...]
  transfers between devices with their start and end apart: 13 -> 0, of which waited for: 10 -> 0; matrix products, arithmetic and copies ran while one was open for 39% -> 0% of each run, Pallas kernels for 0% -> 0%
where the time goes in v1:
time: 322 us; the launch traced here: 321 us
  Pallas kernels  255 us (79%)
  matrix products  36.1 us (11%)
  other arithmetic  19.3 us (6%)
  local copies, waits for them, and re-layouts  9.98 us (3%)
    pallas_call x7, Pallas kernels, exchange(): pl.pallas_call(functools.partial(exchange_kernel, kind, same), out_shape=...  255 us
    dot_general x7, matrix products, dims(): lax.dot_general(a, b, (contract, ((), ())), preferred_element_type=jnp.fl...  18 us
    dot_general x7, matrix products, dot32(): return jnp.dot(a, b, preferred_element_type=jnp.float32)  9.96 us

profile of v1, /device:TPU:0, one launch (start us, length us, event | category | flops | bytes accessed | tf_op | source)
XLA Modules:
  0.0 321.1 jit_solution(11532189939880257325)
XLA Ops:
  0.6 1.0 fusion.140
  1.6 0.9 fusion.86
  2.6 1.1 pad_maximum_fusion.send_ref
  3.7 15.1 %shard_map.129 = bf16[4,256,512]{2,1,0:T(8,128)(2,1)} custom-call(bf16[4,256,512]{2,1,0:T(8,128)(2,1)} %pad_maximum_fusion.send_ref), custom_call_target="tpu_custom_call" | custom-call | tf_op jit(solution)/shard_map/pallas_call | solution.py:81
  18.8 1.3 fusion.135
  20.1 0.0 copy-done.9
  20.2 0.6 fusion.141
  20.7 2.6 compare_select_fusion.1
  23.4 0.5 fusion.142
  23.9 0.2 fusion.79
  24.1 0.0 copy-start.5
  24.1 0.4 fusion.36
  24.6 1.5 copy-done.5
  26.2 5.0 %convolution_convert_fusion = bf16[512,7168]{1,0:T(8,128)(2,1)} fusion(bf16[512,256]{1,0:T(8,128)(2,1)S(1)} %bitcast.238, bf16[256,7168]{1,0:T(8,128)(2,1)S(1)} %copy-done.5), kind=kOutput, calls=%fused_computation | convolution fusion | flops 1882718208 | bytes 11272192 | tf_op jit(solution)/shard_map/dot_general | solution.py:98
  31.2 113.0 %shard_map.130 = bf16[2,256,7168]{2,1,0:T(8,128)(2,1)} custom-call(bf16[2,256,7168]{2,1,0:T(8,128)(2,1)} %bitcast.220), custom_call_target="tpu_custom_call" | custom-call | tf_op jit(solution)/shard_map/pallas_call | solution.py:81
  144.2 6.4 %add_convert_fusion = bf16[1,256,7168]{2,1,0:T(8,128)(2,1)} fusion(bf16[2,256,7168]{2,1,0:T(8,128)(2,1)} %shard_map.130), kind=kLoop, calls=%fused_computation.11 | loop fusion | flops 7340032 | bytes 11010048 | tf_op jit(solution)/shard_map/convert_element_type | solution.py:175
  150.5 58.4 %shard_map.131 = bf16[2,128,7168]{2,1,0:T(8,128)(2,1)} custom-call(bf16[2,128,7168]{2,1,0:T(8,128)(2,1)} %bitcast.221), custom_call_target="tpu_custom_call" | custom-call | tf_op jit(solution)/shard_map/pallas_call | solution.py:81
  208.9 0.0 copy-start.10
  208.9 0.0 copy-start.11
  208.9 0.0 copy-start.3
  208.9 5.1 %convert_reduce_fusion = f32[128,7168]{1,0:T(8,128)} fusion(bf16[2,128,7168]{2,1,0:T(8,128)(2,1)} %shard_map.131), kind=kLoop, calls=%fused_computation.10 | loop fusion | flops 2752512 | bytes 7340032 | tf_op jit(solution)/shard_map/reduce_sum | solution.py:177
  214.0 0.0 copy-done.10
  214.0 0.0 copy-done.11
  214.1 0.1 fusion.95
  214.2 0.1 select_reduce_fusion.1
  214.3 0.1 mul.65
  214.4 0.0 copy-done.3
  214.4 0.4 fusion.4
  214.8 1.1 copy-done.4
  215.9 2.6 convolution_convert_fusion.1
  218.6 0.1 slice_bitcast_fusion.23
  218.7 3.4 %convolution_convert_fusion.7 = bf16[4,896,128]{1,2,0:T(8,128)(2,1)} fusion(bf16[1,32,896]{2,1,0:T(8,128)(2,1)S(1)} %get-tuple-element.57, bf16[1,32,896]{2,1,0:T(8,128)(2,1)S(1)} %get-tuple-element.58, bf16[1,32,896]{2,1,0:T(8,128)(2,1)S(1)} %get-tuple-element.59, bf16[1,32,896]{2,1,0:T(8,128)(2,1)S(1)} %get-tuple-element.60, ...), kind=kOutput, calls=%fused_computation.36 | convolution fusion | flops 132595712 | bytes 1835520 | tf_op jit(solution)/shard_map/pq,gqw->gpw/dot_general | solution.py:191
  222.0 25.1 %shard_map.132 = bf16[32,16,896]{2,1,0:T(8,128)(2,1)} custom-call(bf16[32,16,896]{2,1,0:T(8,128)(2,1)} %bitcast.241), custom_call_target="tpu_custom_call" | custom-call | tf_op jit(solution)/shard_map/pallas_call | solution.py:81
  247.2 0.0 copy-start.1
  247.2 1.7 fusion.28
  248.9 0.1 fusion.136
  249.0 0.5 copy-done.1
  249.5 1.3 fusion.33
  250.8 0.7 copy-done
  251.5 0.7 fusion.30
  252.2 0.8 pad_maximum_fusion.1.send_ref
  253.0 8.1 %shard_map.133 = bf16[4,64,1024]{2,1,0:T(8,128)(2,1)} custom-call(bf16[4,64,1024]{2,1,0:T(8,128)(2,1)} %pad_maximum_fusion.1.send_ref), custom_call_target="tpu_custom_call" | custom-call | tf_op jit(solution)/shard_map/pallas_call | solution.py:81
  261.1 1.1 convert_reduce_fusion.1
  262.3 0.1 multiply_convert_fusion
  262.3 0.7 pad_maximum_fusion.10.send_ref
  263.0 8.5 %shard_map.134 = bf16[4,64,1024]{2,1,0:T(8,128)(2,1)} custom-call(bf16[64,1024]{1,0:T(8,128)(2,1)} %pad_maximum_fusion.10.send_ref), custom_call_target="tpu_custom_call" | custom-call | tf_op jit(solution)/shard_map/pallas_call | solution.py:81
  271.5 1.1 fusion.137
  272.6 0.0 copy-start.2
  272.6 3.5 %fusion.18 = bf16[128,1792]{1,0:T(8,128)(2,1)S(1)} fusion(bf16[128,1024]{1,0:T(8,128)(2,1)S(1)} %bitcast.226, bf16[1,1792,1024]{2,1,0:T(8,128)(2,1)} %param.16), kind=kOutput, calls=%fused_computation.29 | convolution fusion | flops 469991424 | bytes 4390912 | tf_op jit(solution)/shard_map/dot_general | solution.py:102
  276.1 0.0 copy-done.2
  276.2 0.7 fusion.21
  276.9 1.4 convolution_convert_fusion.5
  278.2 26.6 %shard_map.135 = bf16[32,16,896]{2,1,0:T(8,128)(2,1)} custom-call(bf16[32,16,896]{2,1,0:T(8,128)(2,1)} %bitcast.242), custom_call_target="tpu_custom_call" | custom-call | tf_op jit(solution)/shard_map/pallas_call | solution.py:81
  304.8 1.6 fusion.29
  306.6 0.0 copy-start.6
  306.6 0.8 copy-done.6
  307.4 0.8 copy-done.8
  308.2 0.1 eq.103
  308.3 0.1 select_convert_fusion
  308.4 0.0 copy-start.7
  308.4 4.8 %fusion.3 = bf16[1,128,7168]{2,1,0:T(8,128)(2,1)} fusion(f32[128,7168]{1,0:T(8,128)} %convert_reduce_fusion, bf16[1,128,7168]{2,1,0:T(8,128)(2,1)} %param.12, bf16[32,7168]{1,0:T(8,128)(2,1)} %copy-done.8, bf16[32,128]{1,0:T(8,128)(2,1)S(1)} %subtract_convert_fusion, bf16[32,128]{1,0:T(8,128)(2,1)S(1)} %get-tuple-element.18), kind=kOutput, calls=%fused_computation.6 | convolution fusion | flops 124813312 | bytes 7815168 | tf_op jit(solution)/shard_map/dot_general | solution.py:102
  313.2 1.9 fusion.2
  315.1 3.0 fusion.16
  318.1 3.0 fusion.17
  (28 shorter events, 0.4 us)
Async XLA Ops:
  3.7 16.5 %copy-start.9 = (s32[1,4]{1,0:T(1,128)S(1)}, s32[1,4]{1,0:T(1,128)}, u32[]{:S(2)}) copy-start(s32[1,4]{1,0:T(1,128)} %param.21) | copy-start | bytes 52
  24.1 2.0 copy-start.5
  208.9 5.1 %copy-start.10 = (f32[1,128,8]{1,2,0:T(8,128)S(1)}, f32[1,128,8]{1,2,0:T(8,128)}, u32[]{:S(2)}) copy-start(f32[1,128,8]{1,2,0:T(8,128)} %param.20) | copy-start | bytes 12292
  208.9 5.1 %copy-start.11 = (s32[1,128,8]{1,2,0:T(8,128)S(1)}, s32[1,128,8]{1,2,0:T(8,128)}, u32[]{:S(2)}) copy-start(s32[1,128,8]{1,2,0:T(8,128)} %param.19) | copy-start | bytes 12292
  208.9 5.5 %copy-start.3 = (bf16[1,128,7168]{2,1,0:T(8,128)(2,1)S(1)}, bf16[1,128,7168]{2,1,0:T(8,128)(2,1)}, u32[]{:S(2)}) copy-start(bf16[1,128,7168]{2,1,0:T(8,128)(2,1)} %param.18) | copy-start | bytes 5505028
  214.4 1.5 copy-start.4
  247.2 2.3 copy-start.1
  249.5 2.0 copy-start
  272.6 3.6 %copy-start.2 = (bf16[1,1024,1792]{2,1,0:T(8,128)(2,1)S(1)}, bf16[1,1024,1792]{2,1,0:T(8,128)(2,1)}, u32[]{:S(2)}) copy-start(bf16[1,1024,1792]{2,1,0:T(8,128)(2,1)} %param.17) | copy-start | bytes 11010052
  306.6 0.8 copy-start.6
  307.4 0.8 copy-start.8
  308.4 4.8 %copy-start.7 = (bf16[32,7168]{1,0:T(8,128)(2,1)S(1)}, bf16[32,7168]{1,0:T(8,128)(2,1)}, u32[]{:S(2)}) copy-start(bf16[32,7168]{1,0:T(8,128)(2,1)} %copy-done.6) | copy-start | bytes 1376260

commit v2 on v1

--- a/solution.py
+++ b/solution.py
@@ -34,8 +34,12 @@
     return ctx_count // 2, c // 2, lambda j: (j * 2 + c % 2, e)
 
 
-def exchange_kernel(kind, same, send_ref, out_ref, send_sem, recv_sem, own_sem):
-    n, me, place = group_of(kind)
+def exchange_kernel(jobs, *refs):
+    count = len(jobs)
+    sends, outs = refs[:count], refs[count : 2 * count]
+    send_sems, recv_sems = refs[2 * count : 3 * count], refs[3 * count :]
+    widest = "all" if any(kind == "all" for kind, _ in jobs) else jobs[0][0]
+    n, me, place = group_of(widest)
     barrier = pltpu.get_barrier_semaphore()
 
     def greet(k, carry):
@@ -47,51 +51,66 @@
     lax.fori_loop(1, n, greet, 0)
     pl.semaphore_wait(barrier, n - 1)
 
-    def copy_to(k):
-        peer = (me + k) % n
-        return pltpu.make_async_remote_copy(
-            src_ref=send_ref if same else send_ref.at[peer],
-            dst_ref=out_ref.at[me],
-            send_sem=send_sem.at[k],
-            recv_sem=recv_sem.at[k],
-            device_id=place(peer),
-            device_id_type=MESH,
-        )
-
-    def start(k, carry):
-        copy_to(k).start()
-        return carry
-
-    def finish(k, carry):
-        copy_to(k).wait()
-        return carry
-
-    lax.fori_loop(1, n, start, 0)
-    own = pltpu.make_async_copy(
-        send_ref if same else send_ref.at[me], out_ref.at[me], own_sem
-    )
-    own.start()
-    own.wait()
-    lax.fori_loop(1, n, finish, 0)
-
-
-def exchange(kind, send, same, collective_id):
-    n = group_of(kind)[0]
-    block = send.shape if same else send.shape[1:]
+    def copier(job):
+        kind, same = jobs[job]
+        n, me, place = group_of(kind)
+
+        def copy_to(k):
+            peer = (me + k) % n
+            return pltpu.make_async_remote_copy(
+                src_ref=sends[job] if same else sends[job].at[peer],
+                dst_ref=outs[job].at[me],
+                send_sem=send_sems[job].at[k],
+                recv_sem=recv_sems[job].at[k],
+                device_id=place(peer),
+                device_id_type=MESH,
+            )
+
+        def start(k, carry):
+            copy_to(k).start()
+            return carry
+
+        def finish(k, carry):
+            copy_to(k).wait()
+            return carry
+
+        return n, start, finish
+
+    for job in range(count):
+        n, start, _ = copier(job)
+        lax.fori_loop(1, n, start, 0)
+    for job in range(count):
+        n, _, finish = copier(job)
+        lax.fori_loop(1, n, finish, 0)
+
+
+def exchange_raw(jobs, sends, collective_id):
+    sizes = [group_of(kind)[0] for kind, _ in jobs]
+    blocks = [send.shape if same else send.shape[1:] for (_, same), send in zip(jobs, sends)]
     return pl.pallas_call(
-        functools.partial(exchange_kernel, kind, same),
-        out_shape=jax.ShapeDtypeStruct((n,) + tuple(block), send.dtype),
-        in_specs=[pl.BlockSpec(memory_space=pl.ANY)],
-        out_specs=pl.BlockSpec(memory_space=pl.ANY),
-        scratch_shapes=[
-            pltpu.SemaphoreType.DMA((n,)),
-            pltpu.SemaphoreType.DMA((n,)),
-            pltpu.SemaphoreType.DMA,
+        functools.partial(exchange_kernel, tuple(jobs)),
+        out_shape=[
+            jax.ShapeDtypeStruct((n,) + tuple(block), send.dtype)
+            for n, block, send in zip(sizes, blocks, sends)
         ],
+        in_specs=[pl.BlockSpec(memory_space=pl.ANY)] * len(jobs),
+        out_specs=[pl.BlockSpec(memory_space=pl.ANY)] * len(jobs),
+        scratch_shapes=[pltpu.SemaphoreType.DMA((n,)) for n in sizes] * 2,
         compiler_params=pltpu.CompilerParams(
             collective_id=collective_id, has_side_effects=True
         ),
-    )(send)
+    )(*sends)
+
+
+def with_own(kind, same, send, got):
+    n, me, _ = group_of(kind)
+    mine = jnp.arange(n).reshape((n,) + (1,) * (got.ndim - 1)) == me
+    return jnp.where(mine, send[None] if same else send, got)
+
+
+def exchange(kind, send, same, collective_id):
+    (got,) = exchange_raw([(kind, same)], [send], collective_id)
+    return with_own(kind, same, send, got)
 
 
 def dot32(a, b):
@@ -102,11 +121,9 @@
     return lax.dot_general(a, b, (contract, ((), ())), preferred_element_type=jnp.float32)
 
 
-def head_slice(queries, latent, doc_row, width):
+def head_inputs(queries, latent, width):
     ctx_count = lax.axis_size("ctx")
-    tokens = latent.shape[0]
-    length = ctx_count * tokens
-    send = jnp.stack(
+    return jnp.stack(
         [
             jnp.concatenate(
                 [latent, queries[:, (j * width // LAT) * LAT : (j * width // LAT + 1) * LAT]]
@@ -114,7 +131,11 @@
             for j in range(ctx_count)
         ]
     )
-    got = exchange("ctx", send, False, 1)
+
+
+def head_slice(got, doc_row, width):
+    tokens = got.shape[1] // 2
+    length = got.shape[0] * tokens
     keys = got[:, :tokens].reshape(length, LAT)
     asks = got[:, tokens:].reshape(length, LAT)
     positions = jnp.arange(length, dtype=jnp.int32)
@@ -167,57 +188,71 @@
     rows = experts * CAP
     bf16 = jnp.bfloat16
 
+    picker, weigher = slot_tables(routes[0], gate_values[0], experts)
+    picker_half = picker.astype(bf16)
+    slot_gate = jnp.sum(weigher, axis=1)
+    slot_cot = (dot32(picker_half, cotangent[0]) * slot_gate[:, None]).astype(bf16)
+
+    to_row = jnp.arange(experts * MSG, dtype=jnp.int32)
+    from_row = ((to_row % MSG) // CAP) * rows + (to_row // MSG) * CAP + to_row % CAP
+    order = (from_row[:, None] == to_row[None, :]).astype(bf16)
+
+    def pack(pieces):
+        packed = jnp.einsum(
+            "pq,gqw->gpw", order, jnp.concatenate(pieces, axis=1),
+            preferred_element_type=jnp.float32,
+        )
+        return packed.astype(bf16).reshape(ctx_count * experts, MSG, -1)
+
+    def unpack(messages):
+        return jnp.einsum(
+            "qp,gqw->gpw", order, messages.reshape(ctx_count, experts * MSG, -1),
+            preferred_element_type=jnp.float32,
+        ).astype(bf16)
+
+    quarter = part // 4
+
+    def by_part(values):
+        return [
+            jnp.stack(
+                [
+                    values[:, j * part + q * quarter : j * part + (q + 1) * quarter]
+                    for j in range(ctx_count)
+                ]
+            )
+            for q in range(4)
+        ]
+
+    def joined(values):
+        pieces = [
+            values[:, q * rows : (q + 1) * rows].reshape(ctx_count * rows, quarter)
+            for q in range(4)
+        ]
+        return jnp.concatenate(pieces, axis=1)
+
     width = out_proj.shape[0]
-    heads = head_slice(queries[0], latent[0], documents[0], width)
+    head_send = head_inputs(queries[0], latent[0], width)
+    cot_send = pack(by_part(slot_cot))
+    head_got, cot_got = exchange_raw(
+        [("ctx", False), ("all", False)], [head_send, cot_send], 1
+    )
+    cot_rows = joined(unpack(with_own("all", False, cot_send, cot_got)))
+
+    heads = head_slice(with_own("ctx", False, head_send, head_got), documents[0], width)
     heads = heads.reshape(chips, 2, tokens, width).swapaxes(0, 1)
     partial_sums = dot32(heads.reshape(-1, width), out_proj).astype(bf16)
-    paired = exchange("core", partial_sums.reshape(2, chips * tokens, model), False, 2)
-    paired = (paired[0].astype(jnp.float32) + paired[1].astype(jnp.float32)).astype(bf16)
+    partial_sums = partial_sums.reshape(2, chips * tokens, model)
+    (paired,) = exchange_raw([("core", False)], [partial_sums], 2)
+    core = lax.axis_index("ctx") % 2
+    paired = (
+        lax.dynamic_index_in_dim(partial_sums, core, 0, False).astype(jnp.float32)
+        + lax.dynamic_index_in_dim(paired, 1 - core, 0, False).astype(jnp.float32)
+    ).astype(bf16)
     landed = exchange("chip", paired.reshape(chips, tokens, model), False, 3)
     projected = jnp.sum(landed.astype(jnp.float32), axis=0)
     hidden_in = (residual[0].astype(jnp.float32) + projected).astype(bf16)
-
-    picker, weigher = slot_tables(routes[0], gate_values[0], experts)
-    picker_half = picker.astype(bf16)
-    slot_gate = jnp.sum(weigher, axis=1)
     slot_in = dot32(picker_half, hidden_in).astype(bf16)
-    slot_cot = (dot32(picker_half, cotangent[0]) * slot_gate[:, None]).astype(bf16)
-
-    to_row = jnp.arange(experts * MSG, dtype=jnp.int32)
-    from_row = ((to_row % MSG) // CAP) * rows + (to_row // MSG) * CAP + to_row % CAP
-    order = (from_row[:, None] == to_row[None, :]).astype(bf16)
-
-    def pack(first, second):
-        return jnp.einsum(
-            "pq,gqw->gpw", order, jnp.concatenate([first[0], first[1], second[0], second[1]], axis=1),
-            preferred_element_type=jnp.float32,
-        ).astype(bf16).reshape(ctx_count * experts, MSG, half)
-
-    def unpack(messages):
-        return jnp.einsum(
-            "qp,gqw->gpw", order, messages.reshape(ctx_count, experts * MSG, half),
-            preferred_element_type=jnp.float32,
-        ).astype(bf16)
-
-    def by_part(values):
-        return [
-            jnp.stack(
-                [values[:, j * part + h * half : j * part + (h + 1) * half] for j in range(ctx_count)]
-            )
-            for h in range(2)
-        ]
-
-    arrived = unpack(exchange("all", pack(by_part(slot_in), by_part(slot_cot)), False, 4))
-
-    def joined(values, first):
-        pieces = [
-            values[:, (first + h) * rows : (first + h + 1) * rows].reshape(ctx_count * rows, half)
-            for h in range(2)
-        ]
-        return jnp.concatenate(pieces, axis=1)
-
-    in_rows = joined(arrived, 0)
-    cot_rows = joined(arrived, 2)
+    in_rows = joined(unpack(exchange("all", pack(by_part(slot_in)), False, 4)))
     up_part = up_weight[0]
     down_part = down_weight[0]
     hidden = up_part.shape[1]
@@ -245,7 +280,7 @@
         grouped = values.reshape(ctx_count, rows, part)
         return [grouped[:, :, :half], grouped[:, :, half:]]
 
-    back = unpack(exchange("all", pack(halves(slot_out), halves(slot_in_grad)), False, 7))
+    back = unpack(exchange("all", pack(halves(slot_out) + halves(slot_in_grad)), False, 7))
 
     def widened(first):
         return jnp.concatenate(

time: 322 us -> 202 us (0.63)
  Pallas kernels: 255 us -> 134 us
  other arithmetic: 19.3 us -> 24.9 us
  matrix products: 36.1 us -> 30.9 us
    pallas_call x7, Pallas kernels: 255 us -> 134 us  [exchange_raw(): pl.pallas_call(functools.partial(exchange_kernel, tuple(jobs)), out_shape...]
    select_n x0 -> x4, other arithmetic: none -> 5.72 us  [with_own(): return jnp.where(mine, send[None] if same else send, got)]
where the time goes in v2:
time: 202 us; the launch traced here: 201 us
  Pallas kernels  134 us (66%)
  matrix products  30.9 us (15%)
  other arithmetic  24.9 us (12%)
  local copies, waits for them, and re-layouts  10.4 us (5%)
    pallas_call x7, Pallas kernels, exchange_raw(): pl.pallas_call(functools.partial(exchange_kernel, tuple(jobs)), out_shape...  134 us
    dot_general x7, matrix products, dims(): lax.dot_general(a, b, (contract, ((), ())), preferred_element_type=jnp.fl...  16.5 us
    dot_general x7, matrix products, dot32(): return jnp.dot(a, b, preferred_element_type=jnp.float32)  11.3 us
    convert_element_type x1, other arithmetic, shards(): paired = (lax.dynamic_index_in_dim(partial_sums, core, 0, False).astype(j...  6.36 us
    select_n x4, other arithmetic, with_own(): return jnp.where(mine, send[None] if same else send, got)  5.72 us
    reduce_sum x1, other arithmetic, shards(): projected = jnp.sum(landed.astype(jnp.float32), axis=0)  5.02 us
    unnamed x31, local copies, waits for them, and re-layouts  4.23 us

profile of v2, /device:TPU:0, one launch (start us, length us, event | category | flops | bytes accessed | tf_op | source)
XLA Modules:
  0.0 201.5 jit_solution(3854505076049181740)
XLA Ops:
  0.6 0.7 select_reduce_fusion
  1.4 0.1 fusion.131
  1.5 0.1 select_reduce_fusion.1
  1.6 0.1 mul.75
  1.7 1.9 fusion.4
  3.6 0.1 slice_bitcast_fusion.47
  3.8 0.3 fusion.29
  4.1 1.0 copy.74
  5.2 1.1 pad_maximum_fusion.refs_0_
  6.3 26.1 %shard_map.129 = (bf16[4,256,512]{2,1,0:T(8,128)(2,1)}, bf16[32,16,448]{2,1,0:T(8,128)(2,1)}) custom-call(bf16[4,256,512]{2,1,0:T(8,128)(2,1)} %pad_maximum_fusion.refs_0_, bf16[32,16,448]{2,1,0:T(8,128)(2,1)} %bitcast.276), custom_call_target="tpu_custom_call" | custom-call | tf_op jit(solution)/shard_map/pallas_call | solution.py:90
  32.5 1.4 broadcast_select_fusion
  34.0 0.6 fusion.177
  34.6 2.6 %compare_select_fusion.1 = s32[512,1]{0,1:T(1,128)S(1)} fusion(s32[512,1]{0,1:T(1,128)S(1)} %bitcast.318, s32[512,1]{0,1:T(1,128)S(1)} %bitcast.317, s32[]{:T(128)} %bitcast.5, s32[]{:T(128)} %bitcast.6, s32[]{:T(128)} %bitcast.8, s32[]{:T(128)} %bitcast.7), kind=kLoop, calls=%fused_computation.238 | loop fusion | flops 4096 | bytes 6160 | tf_op jit(solution)/shard_map/jit(_take)/gather | solution.py:142
  37.2 0.5 fusion.178
  37.7 0.2 fusion.51
  37.9 0.4 fusion.39
  38.4 1.5 copy-done.7
  40.0 5.0 %convolution_convert_fusion = bf16[512,7168]{1,0:T(8,128)(2,1)} fusion(bf16[512,256]{1,0:T(8,128)(2,1)S(1)} %bitcast.295, bf16[256,7168]{1,0:T(8,128)(2,1)S(1)} %copy-done.7), kind=kOutput, calls=%fused_computation | convolution fusion | flops 1882718208 | bytes 11272192 | tf_op jit(solution)/shard_map/dot_general | solution.py:117
  45.0 6.8 %shard_map.130 = bf16[2,256,7168]{2,1,0:T(8,128)(2,1)} custom-call(bf16[2,256,7168]{2,1,0:T(8,128)(2,1)} %bitcast.272), custom_call_target="tpu_custom_call" | custom-call | tf_op jit(solution)/shard_map/pallas_call | solution.py:90
  51.8 6.4 %add_convert_fusion = bf16[1,256,7168]{2,1,0:T(8,128)(2,1)} fusion(bf16[2,256,7168]{2,1,0:T(8,128)(2,1)} %shard_map.130, s32[]{:T(128)S(6)} %select_n.199, bf16[2,256,7168]{2,1,0:T(8,128)(2,1)} %bitcast.273, s32[]{:T(128)S(6)} %select_n.198), kind=kLoop, calls=%fused_computation.11 | loop fusion | flops 7340032 | bytes 11010056 | tf_op jit(solution)/shard_map/convert_element_type | solution.py:250
  58.2 42.4 %shard_map.131 = bf16[2,128,7168]{2,1,0:T(8,128)(2,1)} custom-call(bf16[2,128,7168]{2,1,0:T(8,128)(2,1)} %bitcast.274), custom_call_target="tpu_custom_call" | custom-call | tf_op jit(solution)/shard_map/pallas_call | solution.py:90
  100.6 5.0 %convert_reduce_fusion = f32[128,7168]{1,0:T(8,128)S(1)} fusion(bf16[2,128,7168]{2,1,0:T(8,128)(2,1)} %bitcast.275, bf16[2,128,7168]{2,1,0:T(8,128)(2,1)} %shard_map.131, pred[2]{0:T(512)(128)(4,1)S(1)} %iota_compare_fusion.8), kind=kLoop, calls=%fused_computation.10 | loop fusion | flops 4587520 | bytes 11010050 | tf_op jit(solution)/shard_map/reduce_sum | solution.py:252
  105.6 1.8 copy-done
  107.4 0.5 convolution_convert_fusion.1
  107.9 0.2 slice_bitcast_fusion.31
  108.1 0.3 fusion.30
  108.5 1.0 copy.78
  109.5 17.5 %shard_map.132 = bf16[32,16,448]{2,1,0:T(8,128)(2,1)} custom-call(bf16[32,16,448]{2,1,0:T(8,128)(2,1)} %bitcast.278), custom_call_target="tpu_custom_call" | custom-call | tf_op jit(solution)/shard_map/pallas_call | solution.py:90
  127.0 1.4 broadcast_select_fusion.3
  128.4 0.3 fusion.31
  128.7 0.4 fusion.174
  129.1 0.2 copy.81
  129.3 0.2 copy.82
  129.5 0.2 copy.83
  129.7 0.2 copy.84
  129.9 0.2 concatenate.50
  130.1 2.7 %fusion.33 = bf16[128,1024]{1,0:T(8,128)(2,1)S(1)} fusion(bf16[128,1792]{1,0:T(8,128)(2,1)S(1)} %concatenate.50, bf16[1,1792,1024]{2,1,0:T(8,128)(2,1)} %param.16), kind=kOutput, calls=%fused_computation.47 | convolution fusion | flops 469893120 | bytes 4390912 | tf_op jit(solution)/shard_map/dot_general | solution.py:117
  132.8 0.3 fusion.32
  133.2 0.4 fusion.175
  133.6 0.2 copy.87
  133.8 0.2 copy.88
  134.0 0.2 copy.89
  134.2 0.2 copy.90
  134.4 0.2 concatenate.51
  134.6 3.3 %fusion.36 = bf16[128,1024]{1,0:T(8,128)(2,1)S(1)} fusion(bf16[128,1792]{1,0:T(8,128)(2,1)S(1)} %concatenate.51, bf16[1,1024,1792]{2,1,0:T(8,128)(2,1)} %param.17), kind=kOutput, calls=%fused_computation.48 | convolution fusion | flops 469893120 | bytes 4390912 | tf_op jit(solution)/shard_map/dot_general | solution.py:121
  137.9 0.8 pad_maximum_fusion.1.refs_0_
  138.8 7.0 %shard_map.133 = bf16[4,64,1024]{2,1,0:T(8,128)(2,1)} custom-call(bf16[4,64,1024]{2,1,0:T(8,128)(2,1)} %pad_maximum_fusion.1.refs_0_), custom_call_target="tpu_custom_call" | custom-call | tf_op jit(solution)/shard_map/pallas_call | solution.py:90
  145.8 1.3 convert_reduce_fusion.1
  147.2 0.7 pad_maximum_fusion.4.refs_0_
  147.9 8.5 %shard_map.134 = bf16[4,64,1024]{2,1,0:T(8,128)(2,1)} custom-call(bf16[64,1024]{1,0:T(8,128)(2,1)} %pad_maximum_fusion.4.refs_0_), custom_call_target="tpu_custom_call" | custom-call | tf_op jit(solution)/shard_map/pallas_call | solution.py:90
  156.3 1.2 broadcast_select_fusion.4
  157.6 3.0 %fusion.17 = bf16[1,1024,1792]{2,1,0:T(8,128)(2,1)} fusion(bf16[128,1024]{1,0:T(8,128)(2,1)S(1)} %bitcast.280, bf16[128,1792]{1,0:T(8,128)(2,1)S(1)} %concatenate.51), kind=kOutput, calls=%fused_computation.28 | convolution fusion | flops 471597056 | bytes 4390912 | tf_op jit(solution)/shard_map/dot_general | solution.py:121
  160.6 3.0 %fusion.16 = bf16[1,1792,1024]{2,1,0:T(8,128)(2,1)} fusion(bf16[128,1792]{1,0:T(8,128)(2,1)S(1)} %concatenate.50, bf16[128,1024]{1,0:T(8,128)(2,1)S(1)} %bitcast.287), kind=kOutput, calls=%fused_computation.27 | convolution fusion | flops 471597056 | bytes 4390912 | tf_op jit(solution)/shard_map/dot_general | solution.py:121
  163.5 0.7 fusion.21
  164.2 1.3 fusion.18
  165.6 0.1 fusion.172
  165.7 1.4 convolution_convert_fusion.5
  167.0 25.8 %shard_map.135 = bf16[32,16,896]{2,1,0:T(8,128)(2,1)} custom-call(bf16[32,16,896]{2,1,0:T(8,128)(2,1)} %bitcast.282), custom_call_target="tpu_custom_call" | custom-call | tf_op jit(solution)/shard_map/pallas_call | solution.py:90
  192.9 1.8 broadcast_select_fusion.1
  194.6 0.4 fusion.28
  195.3 0.1 eq.161
  195.4 1.9 fusion.2
  197.3 0.7 copy-done.1
  198.1 3.4 %fusion.3 = bf16[1,128,7168]{2,1,0:T(8,128)(2,1)} fusion(f32[128,7168]{1,0:T(8,128)S(1)} %copy-done.1, bf16[1,128,7168]{2,1,0:T(8,128)(2,1)} %param.12, bf16[32,7168]{1,0:T(8,128)(2,1)S(1)} %get-tuple-element.27, bf16[32,128]{1,0:T(8,128)(2,1)S(1)} %subtract_convert_fusion, bf16[32,128]{1,0:T(8,128)(2,1)S(1)} %get-tuple-element.22), kind=kOutput, calls=%fused_computation.6 | convolution fusion | flops 124813312 | bytes 7815168 | tf_op jit(solution)/shard_map/dot_general | solution.py:121
  (50 shorter events, 0.6 us)
Async XLA Ops:
  3.8 1.4 copy-start.9
  3.8 1.4 copy-start.10
  5.2 28.8 %copy-start.11 = (s32[1,4]{1,0:T(1,128)S(1)}, s32[1,4]{1,0:T(1,128)}, u32[]{:S(2)}) copy-start(s32[1,4]{1,0:T(1,128)} %param.21) | copy-start | bytes 52
  37.9 2.0 %copy-start.7 = (bf16[256,7168]{1,0:T(8,128)(2,1)S(1)}, bf16[256,7168]{1,0:T(8,128)(2,1)}, u32[]{:S(2)}) copy-start(bf16[256,7168]{1,0:T(8,128)(2,1)} %param.15) | copy-start | bytes 11010052
  100.6 6.8 %copy-start.5 = (bf16[1,128,7168]{2,1,0:T(8,128)(2,1)S(1)}, bf16[1,128,7168]{2,1,0:T(8,128)(2,1)}, u32[]{:S(2)}) copy-start(bf16[1,128,7168]{2,1,0:T(8,128)(2,1)} %param.12) | copy-start | bytes 5505028
  105.6 1.8 copy-start
  108.1 18.9 %copy-start.6 = (bf16[4,128,448]{2,1,0:T(8,128)(2,1)S(1)}, bf16[4,128,448]{2,1,0:T(8,128)(2,1)}, u32[]{:S(2)}) copy-start(bf16[4,128,448]{2,1,0:T(8,128)(2,1)} %copy.74) | copy-start | bytes 1376260
  108.1 18.9 %copy-start.8 = (bf16[32,16,448]{2,1,0:T(8,128)(2,1)S(1)}, bf16[32,16,448]{2,1,0:T(8,128)(2,1)}, u32[]{:S(2)}) copy-start(bf16[32,16,448]{2,1,0:T(8,128)(2,1)} %get-tuple-element.19) | copy-start | bytes 1376260
  157.6 6.0 %copy-start.2 = (bf16[1,1024,1792]{2,1,0:T(8,128)(2,1)S(1)}, bf16[1,1024,1792]{2,1,0:T(8,128)(2,1)}, u32[]{:S(2)}) copy-start(bf16[1,1024,1792]{2,1,0:T(8,128)(2,1)} %param.17) | copy-start | bytes 11010052
  160.6 3.7 %copy-start.3 = (bf16[1,1792,1024]{2,1,0:T(8,128)(2,1)S(1)}, bf16[1,1792,1024]{2,1,0:T(8,128)(2,1)}, u32[]{:S(2)}) copy-start(bf16[1,1792,1024]{2,1,0:T(8,128)(2,1)} %param.16) | copy-start | bytes 11010052
  192.8 2.6 %copy-start.4 = (bf16[1,128,7168]{2,1,0:T(8,128)(2,1)S(1)}, bf16[1,128,7168]{2,1,0:T(8,128)(2,1)}, u32[]{:S(2)}) copy-start(bf16[1,128,7168]{2,1,0:T(8,128)(2,1)} %param.18) | copy-start | bytes 5505028
  195.3 2.7 %copy-start.1 = (f32[128,7168]{1,0:T(8,128)S(1)}, f32[128,7168]{1,0:T(8,128)}, u32[]{:S(2)}) copy-start(f32[128,7168]{1,0:T(8,128)} %copy-done) | copy-start | bytes 11010052

commit v3 on v2

--- a/solution.py
+++ b/solution.py
@@ -233,12 +233,7 @@
     width = out_proj.shape[0]
     head_send = head_inputs(queries[0], latent[0], width)
     cot_send = pack(by_part(slot_cot))
-    head_got, cot_got = exchange_raw(
-        [("ctx", False), ("all", False)], [head_send, cot_send], 1
-    )
-    cot_rows = joined(unpack(with_own("all", False, cot_send, cot_got)))
-
-    heads = head_slice(with_own("ctx", False, head_send, head_got), documents[0], width)
+    heads = head_slice(exchange("ctx", head_send, False, 1), documents[0], width)
     heads = heads.reshape(chips, 2, tokens, width).swapaxes(0, 1)
     partial_sums = dot32(heads.reshape(-1, width), out_proj).astype(bf16)
     partial_sums = partial_sums.reshape(2, chips * tokens, model)
@@ -248,7 +243,12 @@
         lax.dynamic_index_in_dim(partial_sums, core, 0, False).astype(jnp.float32)
         + lax.dynamic_index_in_dim(paired, 1 - core, 0, False).astype(jnp.float32)
     ).astype(bf16)
-    landed = exchange("chip", paired.reshape(chips, tokens, model), False, 3)
+    paired = paired.reshape(chips, tokens, model)
+    landed, cot_got = exchange_raw(
+        [("chip", False), ("all", False)], [paired, cot_send], 3
+    )
+    landed = with_own("chip", False, paired, landed)
+    cot_rows = joined(unpack(with_own("all", False, cot_send, cot_got)))
     projected = jnp.sum(landed.astype(jnp.float32), axis=0)
     hidden_in = (residual[0].astype(jnp.float32) + projected).astype(bf16)
     slot_in = dot32(picker_half, hidden_in).astype(bf16)

time: 202 us -> 212 us (1.050)
  local copies, waits for them, and re-layouts: 10.4 us -> 21.5 us
    slice x10, local copies, waits for them, and re-layouts: 2.39 us -> 10.8 us  [joined(): values[:, q * rows:(q + 1) * rows].reshape(ctx_count * rows, quarter)]
where the time goes in v3:
time: 212 us; the launch traced here: 211 us
  Pallas kernels  134 us (63%)
  matrix products  29.4 us (14%)
  other arithmetic  25.2 us (12%)
  local copies, waits for them, and re-layouts  21.5 us (10%)
    pallas_call x7, Pallas kernels, exchange_raw(): pl.pallas_call(functools.partial(exchange_kernel, tuple(jobs)), out_shape...  134 us
    dot_general x7, matrix products, dims(): lax.dot_general(a, b, (contract, ((), ())), preferred_element_type=jnp.fl...  16.5 us
    slice x10, local copies, waits for them, and re-layouts, joined(): values[:, q * rows:(q + 1) * rows].reshape(ctx_count * rows, quarter)  10.8 us
    dot_general x7, matrix products, dot32(): return jnp.dot(a, b, preferred_element_type=jnp.float32)  9.82 us
    convert_element_type x1, other arithmetic, shards(): paired = (lax.dynamic_index_in_dim(partial_sums, core, 0, False).astype(j...  6.47 us
    select_n x4, other arithmetic, with_own(): return jnp.where(mine, send[None] if same else send, got)  5.75 us
    reduce_sum x1, other arithmetic, shards(): projected = jnp.sum(landed.astype(jnp.float32), axis=0)  5.02 us

profile of v3, /device:TPU:0, one launch (start us, length us, event | category | flops | bytes accessed | tf_op | source)
XLA Modules:
  0.0 211.2 jit_solution(10112902991969566734)
XLA Ops:
  0.7 1.0 fusion.176
  1.7 0.9 fusion.120
  2.6 1.1 pad_maximum_fusion.refs_0_
  3.7 15.1 %shard_map.129 = bf16[4,256,512]{2,1,0:T(8,128)(2,1)} custom-call(bf16[4,256,512]{2,1,0:T(8,128)(2,1)} %pad_maximum_fusion.refs_0_), custom_call_target="tpu_custom_call" | custom-call | tf_op jit(solution)/shard_map/pallas_call | solution.py:90
  18.8 1.4 broadcast_select_fusion
  20.4 0.6 fusion.177
  21.0 2.6 %compare_select_fusion.1 = s32[512,1]{0,1:T(1,128)S(1)} fusion(s32[512,1]{0,1:T(1,128)S(1)} %bitcast.318, s32[512,1]{0,1:T(1,128)S(1)} %bitcast.317, s32[]{:T(128)} %bitcast.5, s32[]{:T(128)} %bitcast.6, s32[]{:T(128)} %bitcast.8, s32[]{:T(128)} %bitcast.7), kind=kLoop, calls=%fused_computation.238 | loop fusion | flops 4096 | bytes 6160 | tf_op jit(solution)/shard_map/jit(_take)/gather | solution.py:142
  23.6 0.5 fusion.178
  24.1 0.2 fusion.51
  24.3 0.4 fusion.39
  24.8 1.3 copy-done.7
  26.1 5.0 %convolution_convert_fusion = bf16[512,7168]{1,0:T(8,128)(2,1)} fusion(bf16[512,256]{1,0:T(8,128)(2,1)S(1)} %bitcast.295, bf16[256,7168]{1,0:T(8,128)(2,1)S(1)} %copy-done.7), kind=kOutput, calls=%fused_computation | convolution fusion | flops 1882718208 | bytes 11272192 | tf_op jit(solution)/shard_map/dot_general | solution.py:117
  31.2 7.1 %shard_map.130 = bf16[2,256,7168]{2,1,0:T(8,128)(2,1)} custom-call(bf16[2,256,7168]{2,1,0:T(8,128)(2,1)} %bitcast.272), custom_call_target="tpu_custom_call" | custom-call | tf_op jit(solution)/shard_map/pallas_call | solution.py:90
  38.3 6.5 %add_convert_fusion = bf16[1,256,7168]{2,1,0:T(8,128)(2,1)} fusion(bf16[2,256,7168]{2,1,0:T(8,128)(2,1)} %shard_map.130, s32[]{:T(128)S(6)} %select_n.193, bf16[2,256,7168]{2,1,0:T(8,128)(2,1)} %bitcast.273, s32[]{:T(128)S(6)} %select_n.192), kind=kLoop, calls=%fused_computation.11 | loop fusion | flops 7340032 | bytes 11010056 | tf_op jit(solution)/shard_map/convert_element_type | solution.py:245
  44.8 0.1 fusion.131
  44.9 0.1 select_reduce_fusion.1
  45.0 0.1 mul.78
  45.1 0.4 fusion.4
  45.5 0.1 slice_bitcast_fusion.47
  45.7 0.3 fusion.29
  46.0 1.0 copy.75
  47.0 53.0 %shard_map.131 = (bf16[2,128,7168]{2,1,0:T(8,128)(2,1)}, bf16[32,16,448]{2,1,0:T(8,128)(2,1)}) custom-call(bf16[2,128,7168]{2,1,0:T(8,128)(2,1)} %bitcast.274, bf16[32,16,448]{2,1,0:T(8,128)(2,1)} %bitcast.278), custom_call_target="tpu_custom_call" | custom-call | tf_op jit(solution)/shard_map/pallas_call | solution.py:90
  100.1 5.0 %convert_reduce_fusion = f32[128,7168]{1,0:T(8,128)S(1)} fusion(bf16[2,128,7168]{2,1,0:T(8,128)(2,1)} %bitcast.275, bf16[2,128,7168]{2,1,0:T(8,128)(2,1)} %get-tuple-element.18, pred[2]{0:T(512)(128)(4,1)S(1)} %iota_compare_fusion.8), kind=kLoop, calls=%fused_computation.10 | loop fusion | flops 4587520 | bytes 11010050 | tf_op jit(solution)/shard_map/reduce_sum | solution.py:252
  105.1 1.8 copy-done
  106.9 0.5 convolution_convert_fusion.1
  107.4 0.1 slice_bitcast_fusion.31
  107.5 0.3 fusion.30
  107.9 1.0 copy.78
  108.9 17.4 %shard_map.132 = bf16[32,16,448]{2,1,0:T(8,128)(2,1)} custom-call(bf16[32,16,448]{2,1,0:T(8,128)(2,1)} %bitcast.276), custom_call_target="tpu_custom_call" | custom-call | tf_op jit(solution)/shard_map/pallas_call | solution.py:90
  126.3 1.5 broadcast_select_fusion.3
  127.8 0.3 fusion.31
  128.2 1.3 fusion.174
  129.5 1.2 copy.81
  130.7 1.2 copy.82
  131.9 0.8 copy.83
  132.7 0.2 copy.84
  132.9 1.1 concatenate.50
  134.1 2.7 %fusion.33 = bf16[128,1024]{1,0:T(8,128)(2,1)S(1)} fusion(bf16[128,1792]{1,0:T(8,128)(2,1)S(1)} %concatenate.50, bf16[1,1792,1024]{2,1,0:T(8,128)(2,1)} %param.16), kind=kOutput, calls=%fused_computation.47 | convolution fusion | flops 469893120 | bytes 4390912 | tf_op jit(solution)/shard_map/dot_general | solution.py:117
  136.8 0.3 fusion.32
  137.1 1.3 fusion.175
  138.4 1.9 copy.87
  140.3 1.9 copy.88
  142.1 0.8 copy.89
  143.0 0.2 copy.90
  143.2 1.2 concatenate.51
  144.4 3.3 %fusion.36 = bf16[128,1024]{1,0:T(8,128)(2,1)S(1)} fusion(bf16[128,1792]{1,0:T(8,128)(2,1)S(1)} %concatenate.51, bf16[1,1024,1792]{2,1,0:T(8,128)(2,1)} %param.17), kind=kOutput, calls=%fused_computation.48 | convolution fusion | flops 469893120 | bytes 4390912 | tf_op jit(solution)/shard_map/dot_general | solution.py:121
  147.8 0.8 pad_maximum_fusion.1.refs_0_
  148.6 7.1 %shard_map.133 = bf16[4,64,1024]{2,1,0:T(8,128)(2,1)} custom-call(bf16[4,64,1024]{2,1,0:T(8,128)(2,1)} %pad_maximum_fusion.1.refs_0_), custom_call_target="tpu_custom_call" | custom-call | tf_op jit(solution)/shard_map/pallas_call | solution.py:90
  155.8 1.3 convert_reduce_fusion.1
  157.2 0.7 pad_maximum_fusion.4.refs_0_
  157.8 8.5 %shard_map.134 = bf16[4,64,1024]{2,1,0:T(8,128)(2,1)} custom-call(bf16[64,1024]{1,0:T(8,128)(2,1)} %pad_maximum_fusion.4.refs_0_), custom_call_target="tpu_custom_call" | custom-call | tf_op jit(solution)/shard_map/pallas_call | solution.py:90
  166.3 1.2 broadcast_select_fusion.4
  167.5 3.0 %fusion.17 = bf16[1,1024,1792]{2,1,0:T(8,128)(2,1)} fusion(bf16[128,1024]{1,0:T(8,128)(2,1)S(1)} %bitcast.280, bf16[128,1792]{1,0:T(8,128)(2,1)S(1)} %concatenate.51), kind=kOutput, calls=%fused_computation.28 | convolution fusion | flops 471597056 | bytes 4390912 | tf_op jit(solution)/shard_map/dot_general | solution.py:121
  170.5 3.0 %fusion.16 = bf16[1,1792,1024]{2,1,0:T(8,128)(2,1)} fusion(bf16[128,1792]{1,0:T(8,128)(2,1)S(1)} %concatenate.50, bf16[128,1024]{1,0:T(8,128)(2,1)S(1)} %bitcast.287), kind=kOutput, calls=%fused_computation.27 | convolution fusion | flops 471597056 | bytes 4390912 | tf_op jit(solution)/shard_map/dot_general | solution.py:121
  173.5 0.7 fusion.21
  174.2 1.3 fusion.18
  175.5 0.1 fusion.172
  175.6 1.4 convolution_convert_fusion.5
  177.0 25.7 %shard_map.135 = bf16[32,16,896]{2,1,0:T(8,128)(2,1)} custom-call(bf16[32,16,896]{2,1,0:T(8,128)(2,1)} %bitcast.282), custom_call_target="tpu_custom_call" | custom-call | tf_op jit(solution)/shard_map/pallas_call | solution.py:90
  202.7 1.6 broadcast_select_fusion.1
  204.3 0.4 fusion.28
  205.1 1.9 fusion.2
  207.0 0.7 copy-done.1
  207.8 3.4 %fusion.3 = bf16[1,128,7168]{2,1,0:T(8,128)(2,1)} fusion(f32[128,7168]{1,0:T(8,128)S(1)} %copy-done.1, bf16[1,128,7168]{2,1,0:T(8,128)(2,1)} %param.12, bf16[32,7168]{1,0:T(8,128)(2,1)S(1)} %get-tuple-element.27, bf16[32,128]{1,0:T(8,128)(2,1)S(1)} %subtract_convert_fusion, bf16[32,128]{1,0:T(8,128)(2,1)S(1)} %get-tuple-element.22), kind=kOutput, calls=%fused_computation.6 | convolution fusion | flops 124813312 | bytes 7815168 | tf_op jit(solution)/shard_map/dot_general | solution.py:121
  (56 shorter events, 0.7 us)
Async XLA Ops:
  0.7 19.6 %copy-start.9 = (pred[4]{0:T(512)(128)(4,1)}, pred[4]{0:T(512)(128)(4,1)S(1)}, u32[]{:S(2)}) copy-start(pred[4]{0:T(512)(128)(4,1)S(1)} %iota_compare_fusion.7) | copy-start | bytes 16
  3.7 16.7 %copy-start.8 = (s32[1,4]{1,0:T(1,128)S(1)}, s32[1,4]{1,0:T(1,128)}, u32[]{:S(2)}) copy-start(s32[1,4]{1,0:T(1,128)} %param.21) | copy-start | bytes 52
  24.1 2.0 copy-start.7
  38.2 6.5 %copy-start.11 = (f32[1,128,8]{1,2,0:T(8,128)S(1)}, f32[1,128,8]{1,2,0:T(8,128)}, u32[]{:S(2)}) copy-start(f32[1,128,8]{1,2,0:T(8,128)} %param.20) | copy-start | bytes 12292
  38.3 6.5 %copy-start.12 = (s32[1,128,8]{1,2,0:T(8,128)S(1)}, s32[1,128,8]{1,2,0:T(8,128)}, u32[]{:S(2)}) copy-start(s32[1,128,8]{1,2,0:T(8,128)} %param.19) | copy-start | bytes 12292
  38.3 6.9 %copy-start.4 = (bf16[1,128,7168]{2,1,0:T(8,128)(2,1)S(1)}, bf16[1,128,7168]{2,1,0:T(8,128)(2,1)}, u32[]{:S(2)}) copy-start(bf16[1,128,7168]{2,1,0:T(8,128)(2,1)} %param.18) | copy-start | bytes 5505028
  100.0 6.8 %copy-start.5 = (bf16[1,128,7168]{2,1,0:T(8,128)(2,1)S(1)}, bf16[1,128,7168]{2,1,0:T(8,128)(2,1)}, u32[]{:S(2)}) copy-start(bf16[1,128,7168]{2,1,0:T(8,128)(2,1)} %param.12) | copy-start | bytes 5505028
  105.1 1.8 copy-start
  107.5 18.8 %copy-start.6 = (bf16[4,128,448]{2,1,0:T(8,128)(2,1)S(1)}, bf16[4,128,448]{2,1,0:T(8,128)(2,1)}, u32[]{:S(2)}) copy-start(bf16[4,128,448]{2,1,0:T(8,128)(2,1)} %copy.75) | copy-start | bytes 1376260
  126.3 3.2 %copy-start.13 = (pred[32]{0:T(512)(128)(4,1)}, pred[32]{0:T(512)(128)(4,1)S(1)}, u32[]{:S(2)}) copy-start(pred[32]{0:T(512)(128)(4,1)S(1)} %iota_compare_fusion.6) | copy-start | bytes 100
  143.2 12.6 %copy-start.10 = (pred[4]{0:T(512)(128)(4,1)S(1)}, pred[4]{0:T(512)(128)(4,1)}, u32[]{:S(2)}) copy-start(pred[4]{0:T(512)(128)(4,1)} %copy-done.9) | copy-start | bytes 16
  167.5 6.0 %copy-start.2 = (bf16[1,1024,1792]{2,1,0:T(8,128)(2,1)S(1)}, bf16[1,1024,1792]{2,1,0:T(8,128)(2,1)}, u32[]{:S(2)}) copy-start(bf16[1,1024,1792]{2,1,0:T(8,128)(2,1)} %param.17) | copy-start | bytes 11010052
  170.5 3.7 %copy-start.3 = (bf16[1,1792,1024]{2,1,0:T(8,128)(2,1)S(1)}, bf16[1,1792,1024]{2,1,0:T(8,128)(2,1)}, u32[]{:S(2)}) copy-start(bf16[1,1792,1024]{2,1,0:T(8,128)(2,1)} %param.16) | copy-start | bytes 11010052
  175.5 27.2 %copy-start.14 = (pred[32]{0:T(512)(128)(4,1)S(1)}, pred[32]{0:T(512)(128)(4,1)}, u32[]{:S(2)}) copy-start(pred[32]{0:T(512)(128)(4,1)} %copy-done.13) | copy-start | bytes 100
  205.0 2.7 %copy-start.1 = (f32[128,7168]{1,0:T(8,128)S(1)}, f32[128,7168]{1,0:T(8,128)}, u32[]{:S(2)}) copy-start(f32[128,7168]{1,0:T(8,128)} %copy-done) | copy-start | bytes 11010052

commit v4 on v2

--- a/solution.py
+++ b/solution.py
@@ -233,16 +233,14 @@
     width = out_proj.shape[0]
     head_send = head_inputs(queries[0], latent[0], width)
     cot_send = pack(by_part(slot_cot))
-    head_got, cot_got = exchange_raw(
-        [("ctx", False), ("all", False)], [head_send, cot_send], 1
-    )
-    cot_rows = joined(unpack(with_own("all", False, cot_send, cot_got)))
-
-    heads = head_slice(with_own("ctx", False, head_send, head_got), documents[0], width)
+    heads = head_slice(exchange("ctx", head_send, False, 1), documents[0], width)
     heads = heads.reshape(chips, 2, tokens, width).swapaxes(0, 1)
     partial_sums = dot32(heads.reshape(-1, width), out_proj).astype(bf16)
     partial_sums = partial_sums.reshape(2, chips * tokens, model)
-    (paired,) = exchange_raw([("core", False)], [partial_sums], 2)
+    paired, cot_got = exchange_raw(
+        [("core", False), ("all", False)], [partial_sums, cot_send], 2
+    )
+    cot_rows = joined(unpack(with_own("all", False, cot_send, cot_got)))
     core = lax.axis_index("ctx") % 2
     paired = (
         lax.dynamic_index_in_dim(partial_sums, core, 0, False).astype(jnp.float32)

time: 202 us -> 204 us (level)
  no operation moved by 1% of the time
where the time goes in v4:
time: 204 us; the launch traced here: 203 us
  Pallas kernels  136 us (67%)
  matrix products  30.9 us (15%)
  other arithmetic  24.9 us (12%)
  local copies, waits for them, and re-layouts  10.2 us (5%)
    pallas_call x7, Pallas kernels, exchange_raw(): pl.pallas_call(functools.partial(exchange_kernel, tuple(jobs)), out_shape...  136 us
    dot_general x7, matrix products, dims(): lax.dot_general(a, b, (contract, ((), ())), preferred_element_type=jnp.fl...  16.5 us
    dot_general x7, matrix products, dot32(): return jnp.dot(a, b, preferred_element_type=jnp.float32)  11.3 us
    convert_element_type x1, other arithmetic, shards(): paired = (lax.dynamic_index_in_dim(partial_sums, core, 0, False).astype(j...  6.36 us
    select_n x4, other arithmetic, with_own(): return jnp.where(mine, send[None] if same else send, got)  5.72 us
    reduce_sum x1, other arithmetic, shards(): projected = jnp.sum(landed.astype(jnp.float32), axis=0)  5.02 us

profile of v4, /device:TPU:0, one launch (start us, length us, event | category | flops | bytes accessed | tf_op | source)
XLA Modules:
  0.0 203.1 jit_solution(8644671011720043155)
XLA Ops:
  0.6 0.7 select_reduce_fusion
  1.4 0.1 fusion.131
  1.5 0.1 select_reduce_fusion.1
  1.6 0.1 mul.78
  1.7 1.9 fusion.4
  3.6 0.1 slice_bitcast_fusion.47
  3.8 0.3 fusion.29
  4.1 1.0 copy.75
  5.2 1.1 pad_maximum_fusion.refs_0_
  6.3 15.1 %shard_map.129 = bf16[4,256,512]{2,1,0:T(8,128)(2,1)} custom-call(bf16[4,256,512]{2,1,0:T(8,128)(2,1)} %pad_maximum_fusion.refs_0_), custom_call_target="tpu_custom_call" | custom-call | tf_op jit(solution)/shard_map/pallas_call | solution.py:90
  21.4 1.4 broadcast_select_fusion
  23.0 0.6 fusion.177
  23.6 2.6 %compare_select_fusion.1 = s32[512,1]{0,1:T(1,128)S(1)} fusion(s32[512,1]{0,1:T(1,128)S(1)} %bitcast.318, s32[512,1]{0,1:T(1,128)S(1)} %bitcast.317, s32[]{:T(128)} %bitcast.5, s32[]{:T(128)} %bitcast.6, s32[]{:T(128)} %bitcast.8, s32[]{:T(128)} %bitcast.7), kind=kLoop, calls=%fused_computation.238 | loop fusion | flops 4096 | bytes 6160 | tf_op jit(solution)/shard_map/jit(_take)/gather | solution.py:142
  26.2 0.5 fusion.178
  26.7 0.2 fusion.51
  26.9 0.4 fusion.39
  27.4 1.3 copy-done.7
  28.7 5.0 %convolution_convert_fusion = bf16[512,7168]{1,0:T(8,128)(2,1)} fusion(bf16[512,256]{1,0:T(8,128)(2,1)S(1)} %bitcast.295, bf16[256,7168]{1,0:T(8,128)(2,1)S(1)} %copy-done.7), kind=kOutput, calls=%fused_computation | convolution fusion | flops 1882718208 | bytes 11272192 | tf_op jit(solution)/shard_map/dot_general | solution.py:117
  33.7 18.6 %shard_map.130 = (bf16[2,256,7168]{2,1,0:T(8,128)(2,1)}, bf16[32,16,448]{2,1,0:T(8,128)(2,1)}) custom-call(bf16[2,256,7168]{2,1,0:T(8,128)(2,1)} %bitcast.272, bf16[32,16,448]{2,1,0:T(8,128)(2,1)} %bitcast.278), custom_call_target="tpu_custom_call" | custom-call | tf_op jit(solution)/shard_map/pallas_call | solution.py:90
  52.4 6.4 %add_convert_fusion = bf16[1,256,7168]{2,1,0:T(8,128)(2,1)} fusion(bf16[2,256,7168]{2,1,0:T(8,128)(2,1)} %get-tuple-element.18, s32[]{:T(128)S(6)} %select_n.199, bf16[2,256,7168]{2,1,0:T(8,128)(2,1)} %bitcast.273, s32[]{:T(128)S(6)} %select_n.192), kind=kLoop, calls=%fused_computation.11 | loop fusion | flops 7340032 | bytes 11010056 | tf_op jit(solution)/shard_map/convert_element_type | solution.py:248
  58.8 42.2 %shard_map.131 = bf16[2,128,7168]{2,1,0:T(8,128)(2,1)} custom-call(bf16[2,128,7168]{2,1,0:T(8,128)(2,1)} %bitcast.274), custom_call_target="tpu_custom_call" | custom-call | tf_op jit(solution)/shard_map/pallas_call | solution.py:90
  101.0 5.0 %convert_reduce_fusion = f32[128,7168]{1,0:T(8,128)S(1)} fusion(bf16[2,128,7168]{2,1,0:T(8,128)(2,1)} %bitcast.275, bf16[2,128,7168]{2,1,0:T(8,128)(2,1)} %shard_map.131, pred[2]{0:T(512)(128)(4,1)S(1)} %iota_compare_fusion.8), kind=kLoop, calls=%fused_computation.10 | loop fusion | flops 4587520 | bytes 11010050 | tf_op jit(solution)/shard_map/reduce_sum | solution.py:250
  106.1 1.8 copy-done
  107.9 0.5 convolution_convert_fusion.1
  108.4 0.2 slice_bitcast_fusion.31
  108.5 0.3 fusion.30
  108.9 1.0 copy.78
  109.9 17.9 %shard_map.132 = bf16[32,16,448]{2,1,0:T(8,128)(2,1)} custom-call(bf16[32,16,448]{2,1,0:T(8,128)(2,1)} %bitcast.276), custom_call_target="tpu_custom_call" | custom-call | tf_op jit(solution)/shard_map/pallas_call | solution.py:90
  127.8 1.4 broadcast_select_fusion.3
  129.2 0.3 fusion.31
  129.5 0.4 fusion.174
  130.0 0.2 copy.81
  130.2 0.2 copy.82
  130.4 0.2 copy.83
  130.6 0.2 copy.84
  130.7 0.2 concatenate.50
  131.0 2.7 %fusion.33 = bf16[128,1024]{1,0:T(8,128)(2,1)S(1)} fusion(bf16[128,1792]{1,0:T(8,128)(2,1)S(1)} %concatenate.50, bf16[1,1792,1024]{2,1,0:T(8,128)(2,1)} %param.16), kind=kOutput, calls=%fused_computation.47 | convolution fusion | flops 469893120 | bytes 4390912 | tf_op jit(solution)/shard_map/dot_general | solution.py:117
  133.7 0.3 fusion.32
  134.0 0.4 fusion.175
  134.4 0.2 copy.87
  134.6 0.2 copy.88
  134.8 0.2 copy.89
  135.0 0.2 copy.90
  135.2 0.2 concatenate.51
  135.4 3.3 %fusion.36 = bf16[128,1024]{1,0:T(8,128)(2,1)S(1)} fusion(bf16[128,1792]{1,0:T(8,128)(2,1)S(1)} %concatenate.51, bf16[1,1024,1792]{2,1,0:T(8,128)(2,1)} %param.17), kind=kOutput, calls=%fused_computation.48 | convolution fusion | flops 469893120 | bytes 4390912 | tf_op jit(solution)/shard_map/dot_general | solution.py:121
  138.8 0.8 pad_maximum_fusion.1.refs_0_
  139.6 7.6 %shard_map.133 = bf16[4,64,1024]{2,1,0:T(8,128)(2,1)} custom-call(bf16[4,64,1024]{2,1,0:T(8,128)(2,1)} %pad_maximum_fusion.1.refs_0_), custom_call_target="tpu_custom_call" | custom-call | tf_op jit(solution)/shard_map/pallas_call | solution.py:90
  147.2 1.3 convert_reduce_fusion.1
  148.6 0.7 pad_maximum_fusion.4.refs_0_
  149.3 8.5 %shard_map.134 = bf16[4,64,1024]{2,1,0:T(8,128)(2,1)} custom-call(bf16[64,1024]{1,0:T(8,128)(2,1)} %pad_maximum_fusion.4.refs_0_), custom_call_target="tpu_custom_call" | custom-call | tf_op jit(solution)/shard_map/pallas_call | solution.py:90
  157.8 1.2 broadcast_select_fusion.4
  159.0 3.0 %fusion.17 = bf16[1,1024,1792]{2,1,0:T(8,128)(2,1)} fusion(bf16[128,1024]{1,0:T(8,128)(2,1)S(1)} %bitcast.280, bf16[128,1792]{1,0:T(8,128)(2,1)S(1)} %concatenate.51), kind=kOutput, calls=%fused_computation.28 | convolution fusion | flops 471597056 | bytes 4390912 | tf_op jit(solution)/shard_map/dot_general | solution.py:121
  162.0 3.0 %fusion.16 = bf16[1,1792,1024]{2,1,0:T(8,128)(2,1)} fusion(bf16[128,1792]{1,0:T(8,128)(2,1)S(1)} %concatenate.50, bf16[128,1024]{1,0:T(8,128)(2,1)S(1)} %bitcast.287), kind=kOutput, calls=%fused_computation.27 | convolution fusion | flops 471597056 | bytes 4390912 | tf_op jit(solution)/shard_map/dot_general | solution.py:121
  165.0 0.7 fusion.21
  165.6 1.3 fusion.18
  167.0 0.1 fusion.172
  167.1 1.4 convolution_convert_fusion.5
  168.5 26.0 %shard_map.135 = bf16[32,16,896]{2,1,0:T(8,128)(2,1)} custom-call(bf16[32,16,896]{2,1,0:T(8,128)(2,1)} %bitcast.282), custom_call_target="tpu_custom_call" | custom-call | tf_op jit(solution)/shard_map/pallas_call | solution.py:90
  194.5 1.8 broadcast_select_fusion.1
  196.3 0.4 fusion.28
  196.9 0.1 eq.161
  197.1 1.9 fusion.2
  199.0 0.7 copy-done.1
  199.7 3.4 %fusion.3 = bf16[1,128,7168]{2,1,0:T(8,128)(2,1)} fusion(f32[128,7168]{1,0:T(8,128)S(1)} %copy-done.1, bf16[1,128,7168]{2,1,0:T(8,128)(2,1)} %param.12, bf16[32,7168]{1,0:T(8,128)(2,1)S(1)} %get-tuple-element.27, bf16[32,128]{1,0:T(8,128)(2,1)S(1)} %subtract_convert_fusion, bf16[32,128]{1,0:T(8,128)(2,1)S(1)} %get-tuple-element.22), kind=kOutput, calls=%fused_computation.6 | convolution fusion | flops 124813312 | bytes 7815168 | tf_op jit(solution)/shard_map/dot_general | solution.py:121
  (50 shorter events, 0.6 us)
Async XLA Ops:
  3.8 1.4 copy-start.9
  3.8 1.4 copy-start.10
  6.3 16.7 %copy-start.11 = (s32[1,4]{1,0:T(1,128)S(1)}, s32[1,4]{1,0:T(1,128)}, u32[]{:S(2)}) copy-start(s32[1,4]{1,0:T(1,128)} %param.21) | copy-start | bytes 52
  26.7 2.0 %copy-start.7 = (bf16[256,7168]{1,0:T(8,128)(2,1)S(1)}, bf16[256,7168]{1,0:T(8,128)(2,1)}, u32[]{:S(2)}) copy-start(bf16[256,7168]{1,0:T(8,128)(2,1)} %param.15) | copy-start | bytes 11010052
  101.0 6.8 %copy-start.5 = (bf16[1,128,7168]{2,1,0:T(8,128)(2,1)S(1)}, bf16[1,128,7168]{2,1,0:T(8,128)(2,1)}, u32[]{:S(2)}) copy-start(bf16[1,128,7168]{2,1,0:T(8,128)(2,1)} %param.12) | copy-start | bytes 5505028
  106.1 1.8 copy-start
  108.5 19.3 %copy-start.6 = (bf16[4,128,448]{2,1,0:T(8,128)(2,1)S(1)}, bf16[4,128,448]{2,1,0:T(8,128)(2,1)}, u32[]{:S(2)}) copy-start(bf16[4,128,448]{2,1,0:T(8,128)(2,1)} %copy.75) | copy-start | bytes 1376260
  108.5 19.3 %copy-start.8 = (bf16[32,16,448]{2,1,0:T(8,128)(2,1)S(1)}, bf16[32,16,448]{2,1,0:T(8,128)(2,1)}, u32[]{:S(2)}) copy-start(bf16[32,16,448]{2,1,0:T(8,128)(2,1)} %get-tuple-element.19) | copy-start | bytes 1376260
  159.0 6.0 %copy-start.2 = (bf16[1,1024,1792]{2,1,0:T(8,128)(2,1)S(1)}, bf16[1,1024,1792]{2,1,0:T(8,128)(2,1)}, u32[]{:S(2)}) copy-start(bf16[1,1024,1792]{2,1,0:T(8,128)(2,1)} %param.17) | copy-start | bytes 11010052
  162.0 3.7 %copy-start.3 = (bf16[1,1792,1024]{2,1,0:T(8,128)(2,1)S(1)}, bf16[1,1792,1024]{2,1,0:T(8,128)(2,1)}, u32[]{:S(2)}) copy-start(bf16[1,1792,1024]{2,1,0:T(8,128)(2,1)} %param.16) | copy-start | bytes 11010052
  194.5 2.6 %copy-start.4 = (bf16[1,128,7168]{2,1,0:T(8,128)(2,1)S(1)}, bf16[1,128,7168]{2,1,0:T(8,128)(2,1)}, u32[]{:S(2)}) copy-start(bf16[1,128,7168]{2,1,0:T(8,128)(2,1)} %param.18) | copy-start | bytes 5505028
  197.0 2.7 %copy-start.1 = (f32[128,7168]{1,0:T(8,128)S(1)}, f32[128,7168]{1,0:T(8,128)}, u32[]{:S(2)}) copy-start(f32[128,7168]{1,0:T(8,128)} %copy-done) | copy-start | bytes 11010052
